TPU v7x, 256 devices: a whole 4x4x8 slice. The times are simulated.
256 devices in a mesh: mem: 128 (over z, y, x), rep: 2 (over core).
Axes of the slice: x: 4, y: 4, z: 8, core: 2. Of those that a mesh axis runs over, the one named last changes fastest.
Arguments:
- particle_vectors: bfloat16 [512, 131072], P('mem', 'rep'), may hold values from -6 to 6
- observed: bfloat16 [512, 131072], P('mem', 'rep'), may hold values from -24 to 24
- precision: float32 [131072], P('rep'), may hold values from 0.5 to 240, as said below
- entry_projection_matrix: bfloat16 [2, 256, 1024], replicated, may hold values from -0.375 to 0.375
- entry_offsets: float32 [2, 1024], replicated, may hold values from -3 to 3
- exit_projection_matrix: bfloat16 [2, 1024, 256], replicated, may hold values from -0.1875 to 0.1875
- exit_offsets: float32 [2, 256], replicated, may hold values from -3 to 3
Outputs:
- updated: bfloat16 [512, 131072], P('mem', 'rep')
Inputs may be any that keep to these rules, and one draw needn't show every extreme that they name: `precision`: positive precisions.
All inputs are finite; a program needn't handle non-finite values.
Results may differ from a plain program's by a relative error of at most 0.0065.
Values may be sent and summed in bfloat16 or wider, within the bound.
A program may use at most 64 MiB of HBM per device.

v0:
```python
import jax
import jax.numpy as jnp
from jax import lax
from jax.sharding import Mesh
from jax.sharding import PartitionSpec as P

PW = 256
LAYERS = 2
MEM = ("mem_0", "mem_1", "mem_2")


def copy_for_each(array, axis):
    copies = jnp.broadcast_to(array, (lax.axis_size(axis), *array.shape))
    return lax.all_to_all(copies, axis, split_axis=0, concat_axis=0, tiled=True)


def over_copies(array, axis):
    return copy_for_each(array, axis).sum(axis=0)


def one_axis_at_a_time(array, axes):
    far, near = axes
    return over_copies(over_copies(array, near), far)


def cut_along(array, dim, length):
    lengths = array.shape
    pieces = array.reshape(*lengths[:dim], length, lengths[dim] // length, *lengths[dim + 1 :])
    return jnp.moveaxis(pieces, dim, 0)


def sent_and_summed(array, axis, dim):
    length = lax.axis_size(axis)
    pieces = lax.all_to_all(cut_along(array, dim, length), axis, 0, 0, tiled=True)
    return jnp.sum(pieces, axis=0)


def sum_by_axis(array, axes, dim):
    far, near = axes
    own = sent_and_summed(cut_along(array, dim, lax.axis_size(far)), near, dim + 1)
    return jnp.sum(lax.all_to_all(own, far, 0, 0, tiled=True), axis=0)


def laid_out(pieces, dim):
    pieces = jnp.moveaxis(pieces, 0, dim)
    lengths = pieces.shape
    return pieces.reshape(*lengths[:dim], lengths[dim] * lengths[dim + 1], *lengths[dim + 2 :])


def whole_of(array, axes, dim):
    far, near = axes
    leading = copy_for_each(array, far)
    pieces = jnp.swapaxes(copy_for_each(leading, near), 0, 1)
    return laid_out(pieces.reshape(-1, *array.shape), dim)


def contract(left, right):
    return lax.dot_general(
        left, right, (((1,), (1,)), ((), ())), preferred_element_type=jnp.float32
    )


def body(
    particle_vectors,
    observed,
    precision,
    entry_projection_matrix,
    entry_offsets,
    exit_projection_matrix,
    exit_offsets,
):
    owned, local_width = particle_vectors.shape
    stream = particle_vectors.reshape(owned * local_width // PW, PW)
    for layer in range(LAYERS):
        pre = (
            jnp.dot(stream, entry_projection_matrix[layer], preferred_element_type=jnp.float32)
            + entry_offsets[layer]
        )
        hidden = jax.nn.silu(pre).astype(jnp.bfloat16)
        stream = (
            stream.astype(jnp.float32)
            + jnp.dot(hidden, exit_projection_matrix[layer], preferred_element_type=jnp.float32)
            + exit_offsets[layer]
        ).astype(jnp.bfloat16)
    particle_outcomes = stream.reshape(owned, local_width)
    resid = (observed.astype(jnp.float32) - particle_outcomes.astype(jnp.float32)).astype(
        jnp.bfloat16
    )
    resid_wide = resid.astype(jnp.float32)
    mem_count = lax.axis_size(MEM)
    member_total = owned * mem_count
    state_total = local_width * lax.axis_size("rep")
    misfit_local = jnp.sum(resid_wide * resid_wide * precision)
    damping = (
        one_axis_at_a_time(misfit_local, (("mem_0", "mem_1"), ("mem_2", "rep")))
        / (member_total * state_total)
        + 1e-06
    )
    own_states, own_preds, own_resid = (
        lax.all_to_all(particle_vectors, MEM, split_axis=1, concat_axis=0, tiled=True),
        lax.all_to_all(particle_outcomes, MEM, split_axis=1, concat_axis=0, tiled=True),
        lax.all_to_all(resid, MEM, split_axis=1, concat_axis=0, tiled=True),
    )
    block_width = own_states.shape[1]
    prec_block = lax.dynamic_slice_in_dim(precision, lax.axis_index(MEM) * block_width, block_width)
    pred_wide = own_preds.astype(jnp.float32)
    pred_dev = (pred_wide - jnp.mean(pred_wide, axis=0)).astype(jnp.bfloat16)
    state_wide = own_states.astype(jnp.float32)
    state_dev = (state_wide - jnp.mean(state_wide, axis=0)).astype(jnp.bfloat16)
    weighted = (pred_dev.astype(jnp.float32) * prec_block).astype(jnp.bfloat16)
    joint = sum_by_axis(
        jnp.concatenate([contract(weighted, pred_dev), contract(own_resid, weighted)], axis=1),
        (("mem_0", "mem_1"), ("mem_2", "rep")),
        0,
    )
    gram = (
        whole_of(joint[:, :member_total], (("mem_0", "mem_1"), ("mem_2", "rep")), 0) / state_total
    )
    cross = joint[:, member_total:] / state_total
    kmat = gram + damping * jnp.eye(member_total, dtype=jnp.float32)
    factor = jnp.linalg.cholesky(kmat)
    middle = jax.scipy.linalg.solve_triangular(factor, cross.T, lower=True)
    solved = jax.scipy.linalg.solve_triangular(factor, middle, lower=True, trans="T")
    mixing = solved.T.astype(jnp.bfloat16)
    fresh = (
        state_wide
        + jnp.dot(
            whole_of(mixing, (("mem_0", "mem_1"), ("mem_2", "rep")), 0),
            state_dev,
            preferred_element_type=jnp.float32,
        )
    ).astype(jnp.bfloat16)
    return lax.all_to_all(fresh, MEM, split_axis=0, concat_axis=1, tiled=True)


def solution(mesh):
    torus = Mesh(
        mesh.devices.reshape(8, 4, 4, mesh.shape["rep"]), ("mem_0", "mem_1", "mem_2", "rep")
    )
    return jax.shard_map(
        body,
        mesh=torus,
        in_specs=(P(MEM, "rep"), P(MEM, "rep"), P("rep"), P(), P(), P(), P()),
        out_specs=P(MEM, "rep"),
        check_vma=False,
    )
```

profile of v0, /device:TPU:8, one launch (start us, length us, event | category | flops | bytes accessed | tf_op | source)
XLA Modules:
  0.0 406.8 jit_solution(11366948258515956101)
XLA Ops:
  9.6 15.3 %all-to-all-start.1 = ((bf16[4,128,512]{2,0,1:T(4,128)(2,1)}), bf16[4,128,512]{2,0,1:T(4,128)(2,1)S(1)}, u32[]{:S(2)}, u32[]{:S(2)}) async-start(bf16[4,128,512]{2,0,1:T(4,128)(2,1)} %copy.71), calls=%async_computation.1 | async-start | bytes 1048576 | tf_op jit(solution)/shard_map/all_to_all | solution.py:101
  27.4 17.7 %all-to-all-done.1 = bf16[4,128,512]{2,0,1:T(4,128)(2,1)S(1)} async-done(((bf16[4,128,512]{2,0,1:T(4,128)(2,1)}), bf16[4,128,512]{2,0,1:T(4,128)(2,1)S(1)}, u32[]{:S(2)}, u32[]{:S(2)}) %all-to-all-start.1) | async-done | bytes 524320 | tf_op jit(solution)/shard_map/all_to_all | solution.py:101
  45.1 6.6 %all-to-all-start.2 = ((bf16[4,128,512]{2,0,1:T(4,128)(2,1)}), bf16[4,128,512]{2,0,1:T(4,128)(2,1)S(1)}, u32[]{:S(2)}, u32[]{:S(2)}) async-start(bf16[4,128,512]{2,0,1:T(4,128)(2,1)} %bitcast.11), calls=%async_computation.2 | async-start | bytes 1048576 | tf_op jit(solution)/shard_map/all_to_all | solution.py:102
  52.7 17.8 %all-to-all-done.2 = bf16[4,128,512]{2,0,1:T(4,128)(2,1)S(1)} async-done(((bf16[4,128,512]{2,0,1:T(4,128)(2,1)}), bf16[4,128,512]{2,0,1:T(4,128)(2,1)S(1)}, u32[]{:S(2)}, u32[]{:S(2)}) %all-to-all-start.2) | async-done | bytes 524320 | tf_op jit(solution)/shard_map/all_to_all | solution.py:102
  88.8 26.6 %all-to-all-done.3 = f32[8,32,2,1024]{3,2,1,0:T(2,128)S(1)} async-done(((f32[8,32,2,1024]{3,2,1,0:T(2,128)}), f32[8,32,2,1024]{3,2,1,0:T(2,128)S(1)}, u32[]{:S(2)}, u32[]{:S(2)}) %all-to-all-start.3) | async-done | bytes 2097184 | tf_op jit(solution)/shard_map/all_to_all | solution.py:34
  122.4 7.6 %all-to-all-done.8 = f32[32,1,1]{2,1,0:T(1,128)S(1)} async-done(((f32[32,1,1]{2,1,0:T(1,128)}), f32[32,1,1]{2,1,0:T(1,128)S(1)}, u32[]{:S(2)}, u32[]{:S(2)}) %all-to-all-start.8) | async-done | bytes 160 | tf_op jit(solution)/shard_map/all_to_all | solution.py:14
  130.1 14.3 %all_to_all.106 = f32[32,2,1024]{2,1,0:T(2,128)S(1)} all-to-all(f32[32,2,1024]{2,1,0:T(2,128)S(1)} %reduce_sum.64), channel_id=1, replica_groups=mesh['mem_0'=8,'mem_1'=4,'mem_2'=4,'rep'=2] {'mem_0','mem_1'}, dimensions={0} | all-to-all | bytes 524288 | tf_op jit(solution)/shard_map/all_to_all | solution.py:41
  144.4 7.4 %all-to-all-start = ((bf16[4,128,512]{2,0,1:T(4,128)(2,1)}), bf16[4,128,512]{2,0,1:T(4,128)(2,1)S(1)}, u32[]{:S(2)}, u32[]{:S(2)}) async-start(bf16[4,128,512]{2,0,1:T(4,128)(2,1)} %bitcast), calls=%async_computation | async-start | bytes 1048576 | tf_op jit(solution)/shard_map/all_to_all | solution.py:100
  151.8 18.0 %all-to-all-done = bf16[4,128,512]{2,0,1:T(4,128)(2,1)S(1)} async-done(((bf16[4,128,512]{2,0,1:T(4,128)(2,1)}), bf16[4,128,512]{2,0,1:T(4,128)(2,1)S(1)}, u32[]{:S(2)}, u32[]{:S(2)}) %all-to-all-start) | async-done | bytes 524320 | tf_op jit(solution)/shard_map/all_to_all | solution.py:100
  169.9 12.9 %all_to_all.107 = f32[32,2,512]{2,1,0:T(2,128)S(1)} all-to-all(f32[32,2,512]{2,1,0:T(2,128)S(1)} %broadcast_in_dim.24), channel_id=1, replica_groups=mesh['mem_0'=8,'mem_1'=4,'mem_2'=4,'rep'=2] {'mem_0','mem_1'}, dimensions={0} | all-to-all | bytes 262144 | tf_op jit(solution)/shard_map/all_to_all | solution.py:14
  189.4 14.1 %all-to-all-done.6 = f32[8,32,2,512]{3,2,1,0:T(2,128)S(1)} async-done(((f32[8,32,2,512]{3,2,1,0:T(2,128)}), f32[8,32,2,512]{3,2,1,0:T(2,128)S(1)}, u32[]{:S(2)}, u32[]{:S(2)}) %all-to-all-start.6) | async-done | bytes 1048608 | tf_op jit(solution)/shard_map/all_to_all | solution.py:14
  208.7 11.7 %cholesky.103 = f32[128,128]{1,0:T(8,128)S(1)} custom-call(f32[128,128]{1,0:T(8,128)S(1)} %cholesky.263), custom_call_target="Cholesky" | custom-call | tf_op jit(solution)/shard_map/jit(cholesky)/cholesky | solution.py:121
  220.4 9.8 %custom-call.34 = f32[1,128,128]{1,2,0:T(8,128)S(1)} custom-call(f32[1,128,128]{2,1,0:T(8,128)S(1)} %get-tuple-element.52), custom_call_target="InvertDiagBlocksLowerTriangular" | custom-call | tf_op jit(solution)/shard_map/jit(cholesky)/cholesky | solution.py:121
  230.9 11.9 %cholesky.215 = f32[128,128]{1,0:T(8,128)S(1)} custom-call(f32[128,128]{1,0:T(8,128)S(1)} %cholesky.267), custom_call_target="Cholesky" | custom-call | tf_op jit(solution)/shard_map/jit(cholesky)/cholesky | solution.py:121
  243.3 9.8 %custom-call.35 = f32[1,128,128]{1,2,0:T(8,128)S(1)} custom-call(f32[1,128,128]{2,1,0:T(8,128)S(1)} %get-tuple-element.50), custom_call_target="InvertDiagBlocksLowerTriangular" | custom-call | tf_op jit(solution)/shard_map/jit(cholesky)/cholesky | solution.py:121
  255.0 11.7 %cholesky.236 = f32[128,128]{1,0:T(8,128)S(1)} custom-call(f32[128,128]{1,0:T(8,128)S(1)} %cholesky.272), custom_call_target="Cholesky" | custom-call | tf_op jit(solution)/shard_map/jit(cholesky)/cholesky | solution.py:121
  266.9 9.8 %custom-call.36 = f32[1,128,128]{1,2,0:T(8,128)S(1)} custom-call(f32[1,128,128]{2,1,0:T(8,128)S(1)} %get-tuple-element.48), custom_call_target="InvertDiagBlocksLowerTriangular" | custom-call | tf_op jit(solution)/shard_map/jit(cholesky)/cholesky | solution.py:121
  278.3 12.0 %cholesky.253 = f32[128,128]{1,0:T(8,128)S(1)} custom-call(f32[128,128]{1,0:T(8,128)S(1)} %convolution_subtract_fusion.2), custom_call_target="Cholesky" | custom-call | tf_op jit(solution)/shard_map/jit(cholesky)/cholesky | solution.py:121
  295.1 8.9 %while.1 = (s32[]{:T(128)}, f32[512,512]{0,1:T(8,128)S(1)}, s32[4,2]{0,1:T(2,128)S(1)}, f32[4,128,128]{2,1,0:T(8,128)S(1)}, s32[]{:T(128)}) while((s32[]{:T(128)}, f32[512,512]{0,1:T(8,128)S(1)}, s32[4,2]{0,1:T(2,128)S(1)}, f32[4,128,128]{2,1,0:T(8,128)S(1)}, s32[]{:T(128)}) %tuple.36), condition=%wide.while_cond, body=%wide.while_body.sunk | while | flops 2 | bytes 393321 | solution.py:123
  304.1 39.3 %custom-call.37 = f32[4,128,128]{1,2,0:T(8,128)S(1)} custom-call(f32[4,128,128]{2,1,0:T(8,128)S(1)} %get-tuple-element.12), custom_call_target="InvertDiagBlocksLowerTriangular" | custom-call | tf_op jit(solution)/shard_map/jit(_solve_triangular)/triangular_solve | solution.py:123
  347.0 5.4 %all-to-all-start.9 = ((bf16[32,2,512]{2,1,0:T(2,128)(2,1)}), bf16[32,2,512]{2,1,0:T(2,128)(2,1)S(1)}, u32[]{:S(2)}, u32[]{:S(2)}) async-start(bf16[32,2,512]{2,1,0:T(2,128)(2,1)} %broadcast_in_dim.28), calls=%async_computation.9 | async-start | bytes 131072 | tf_op jit(solution)/shard_map/all_to_all | solution.py:14
  352.4 8.8 %all-to-all-done.9 = bf16[32,2,512]{2,1,0:T(2,128)(2,1)S(1)} async-done(((bf16[32,2,512]{2,1,0:T(2,128)(2,1)}), bf16[32,2,512]{2,1,0:T(2,128)(2,1)S(1)}, u32[]{:S(2)}, u32[]{:S(2)}) %all-to-all-start.9) | async-done | bytes 65568 | tf_op jit(solution)/shard_map/all_to_all | solution.py:14
  367.3 9.5 %all-to-all-done.10 = bf16[8,32,2,512]{3,2,1,0:T(2,128)(2,1)} async-done(((bf16[8,32,2,512]{3,2,1,0:T(2,128)(2,1)}), bf16[8,32,2,512]{3,2,1,0:T(2,128)(2,1)}, u32[]{:S(2)}, u32[]{:S(2)}) %all-to-all-start.10) | async-done | bytes 524320 | tf_op jit(solution)/shard_map/all_to_all | solution.py:14
  379.2 26.4 %all_to_all.108 = bf16[128,4,512]{2,1,0:T(4,128)(2,1)S(1)} all-to-all(bf16[128,4,512]{2,1,0:T(4,128)(2,1)S(1)} %all_to_all.90), channel_id=1, replica_groups=mesh['mem_0'=8,'mem_1'=4,'mem_2'=4,'rep'=2] {'mem_0','mem_1','mem_2'}, dimensions={0} | all-to-all | bytes 1048576 | tf_op jit(solution)/shard_map/all_to_all | solution.py:133
  (130 shorter events, 78.0 us)
Async XLA Ops:
  3.0 2.7 copy-start.3
  8.4 17.1 %copy-start.1 = (bf16[4,65536]{1,0:T(4,128)(2,1)S(1)}, bf16[4,65536]{1,0:T(4,128)(2,1)}, u32[]{:S(2)}) copy-start(bf16[4,65536]{1,0:T(4,128)(2,1)} %param.8) | copy-start | bytes 1572868
  8.4 17.1 %copy-start.2 = (f32[65536]{0:T(1024)S(1)}, f32[65536]{0:T(1024)}, u32[]{:S(2)}) copy-start(f32[65536]{0:T(1024)} %param.9) | copy-start | bytes 786436
  9.6 35.5 %all-to-all-start.1 = ((bf16[4,128,512]{2,0,1:T(4,128)(2,1)}), bf16[4,128,512]{2,0,1:T(4,128)(2,1)S(1)}, u32[]{:S(2)}, u32[]{:S(2)}) async-start(bf16[4,128,512]{2,0,1:T(4,128)(2,1)} %copy.71), calls=%async_computation.1 | async-start | bytes 1048576 | tf_op jit(solution)/shard_map/all_to_all | solution.py:101
  45.1 25.4 %all-to-all-start.2 = ((bf16[4,128,512]{2,0,1:T(4,128)(2,1)}), bf16[4,128,512]{2,0,1:T(4,128)(2,1)S(1)}, u32[]{:S(2)}, u32[]{:S(2)}) async-start(bf16[4,128,512]{2,0,1:T(4,128)(2,1)} %bitcast.11), calls=%async_computation.2 | async-start | bytes 1048576 | tf_op jit(solution)/shard_map/all_to_all | solution.py:102
  71.8 11.7 %all-to-all-start.7 = ((f32[8,1,1]{2,1,0:T(1,128)}), f32[8,1,1]{2,1,0:T(1,128)S(1)}, u32[]{:S(2)}, u32[]{:S(2)}) async-start(f32[8,1,1]{2,1,0:T(1,128)} %broadcast_in_dim.26), calls=%async_computation.7 | async-start | bytes 8192 | tf_op jit(solution)/shard_map/all_to_all | solution.py:14
  83.4 32.0 %all-to-all-start.3 = ((f32[8,32,2,1024]{3,2,1,0:T(2,128)}), f32[8,32,2,1024]{3,2,1,0:T(2,128)S(1)}, u32[]{:S(2)}, u32[]{:S(2)}) async-start(f32[8,32,2,1024]{3,2,1,0:T(2,128)} %copy.74), calls=%async_computation.3 | async-start | bytes 4194304 | tf_op jit(solution)/shard_map/all_to_all | solution.py:34
  116.6 13.4 %all-to-all-start.8 = ((f32[32,1,1]{2,1,0:T(1,128)}), f32[32,1,1]{2,1,0:T(1,128)S(1)}, u32[]{:S(2)}, u32[]{:S(2)}) async-start(f32[32,1,1]{2,1,0:T(1,128)} %broadcast_in_dim.27), calls=%async_computation.8 | async-start | bytes 32768 | tf_op jit(solution)/shard_map/all_to_all | solution.py:14
  144.4 25.5 %all-to-all-start = ((bf16[4,128,512]{2,0,1:T(4,128)(2,1)}), bf16[4,128,512]{2,0,1:T(4,128)(2,1)S(1)}, u32[]{:S(2)}, u32[]{:S(2)}) async-start(bf16[4,128,512]{2,0,1:T(4,128)(2,1)} %bitcast), calls=%async_computation | async-start | bytes 1048576 | tf_op jit(solution)/shard_map/all_to_all | solution.py:100
  184.1 19.4 %all-to-all-start.6 = ((f32[8,32,2,512]{3,2,1,0:T(2,128)}), f32[8,32,2,512]{3,2,1,0:T(2,128)S(1)}, u32[]{:S(2)}, u32[]{:S(2)}) async-start(f32[8,32,2,512]{3,2,1,0:T(2,128)} %broadcast_in_dim.25), calls=%async_computation.6 | async-start | bytes 2097152 | tf_op jit(solution)/shard_map/all_to_all | solution.py:14
  208.6 34.4 %copy-start = (f32[512,512]{1,0:T(8,128)}, f32[512,512]{1,0:T(8,128)S(1)}, u32[]{:S(2)}) copy-start(f32[512,512]{1,0:T(8,128)S(1)} %fusion.7) | copy-start | bytes 3145732
  347.0 14.2 %all-to-all-start.9 = ((bf16[32,2,512]{2,1,0:T(2,128)(2,1)}), bf16[32,2,512]{2,1,0:T(2,128)(2,1)S(1)}, u32[]{:S(2)}, u32[]{:S(2)}) async-start(bf16[32,2,512]{2,1,0:T(2,128)(2,1)} %broadcast_in_dim.28), calls=%async_computation.9 | async-start | bytes 131072 | tf_op jit(solution)/shard_map/all_to_all | solution.py:14
  362.3 14.5 %all-to-all-start.10 = ((bf16[8,32,2,512]{3,2,1,0:T(2,128)(2,1)}), bf16[8,32,2,512]{3,2,1,0:T(2,128)(2,1)}, u32[]{:S(2)}, u32[]{:S(2)}) async-start(bf16[8,32,2,512]{3,2,1,0:T(2,128)(2,1)} %broadcast_in_dim.29), calls=%async_computation.10 | async-start | bytes 1048576 | tf_op jit(solution)/shard_map/all_to_all | solution.py:14
where the time goes:
time: 415 us; the launch traced here: 407 us
  other arithmetic  126 us (30%)
  waiting for transfers between devices  120 us (29%)
  starting transfers between devices  56 us (13%)
  blocking collectives  53.7 us (13%)
  local copies, waits for them, and re-layouts  33.1 us (8%)
  matrix products  13.5 us (3%)
  between operations  4.21 us (1%)
    another operation x14, other arithmetic, body(): factor = jnp.linalg.cholesky(kmat)  78.9 us
    all_to_all x5, waiting for transfers between devices, copy_for_each(): return lax.all_to_all(copies, axis, split_axis=0, concat_axis=0, tiled=True)  40 us
    another operation x3, other arithmetic, body(): jax.scipy.linalg.solve_triangular(factor, middle, lower=True, trans='T')  39.4 us
    all_to_all x1, waiting for transfers between devices, sent_and_summed(): lax.all_to_all(cut_along(array, dim, length), axis, 0, 0, tiled=True)  26.6 us
    all_to_all x1, blocking collectives, body(): return lax.all_to_all(fresh, MEM, split_axis=0, concat_axis=1, tiled=True)  26.4 us
    all_to_all x5, starting transfers between devices, copy_for_each(): return lax.all_to_all(copies, axis, split_axis=0, concat_axis=0, tiled=True)  21.9 us
    all_to_all x1, waiting for transfers between devices, body(): lax.all_to_all(particle_vectors, MEM, split_axis=1, concat_axis=0, tiled=...  18 us
    all_to_all x1, waiting for transfers between devices, body(): lax.all_to_all(resid, MEM, split_axis=1, concat_axis=0, tiled=True)  17.8 us
  transfers between devices with their start and end apart: 9, of which 8 were waited for; matrix products, arithmetic and copies ran while one was open for 4% of the time, Pallas kernels for 0%

commit v1 on v0

--- a/solution.py
+++ b/solution.py
@@ -1,6 +1,8 @@
 import jax
 import jax.numpy as jnp
 from jax import lax
+from jax.experimental import pallas as pl
+from jax.experimental.pallas import tpu as pltpu
 from jax.sharding import Mesh
 from jax.sharding import PartitionSpec as P
 
@@ -60,6 +62,69 @@
     )
 
 
+F32 = jnp.float32
+TILE = 128
+
+
+def exact_dot(left, right):
+    return jnp.dot(left, right, precision=lax.Precision.HIGHEST, preferred_element_type=F32)
+
+
+def eliminate(a, first):
+    sub = lax.broadcasted_iota(jnp.int32, (8, TILE), 0)
+    lane = lax.broadcasted_iota(jnp.int32, (8, TILE), 1)
+    rows = a[first : first + 8, :]
+    own = (lane >= first) & (lane < first + 8)
+    fresh = jnp.where(own, jnp.where(lane - first == sub, 1.0, 0.0), rows)
+    cols = [jnp.broadcast_to(rows[:, first + j : first + j + 1], (8, TILE)) for j in range(8)]
+    for k in range(8):
+        inverse = 1.0 / jnp.broadcast_to(cols[k][k : k + 1, :], (8, TILE))
+        row = jnp.broadcast_to(fresh[k : k + 1, :], (8, TILE)) * inverse
+        fresh = jnp.where(sub == k, row, fresh - cols[k] * row)
+        for j in range(k + 1, 8):
+            entry = jnp.broadcast_to(cols[j][k : k + 1, :], (8, TILE)) * inverse
+            cols[j] = jnp.where(sub == k, entry, cols[j] - cols[k] * entry)
+    lanes = lax.broadcasted_iota(jnp.int32, (TILE, TILE), 1)
+    rest = jnp.where((lanes >= first) & (lanes < first + 8), 0.0, a)
+    for j in range(8):
+        left = jnp.broadcast_to(a[:, first + j : first + j + 1], (TILE, TILE))
+        rest = rest - left * jnp.broadcast_to(fresh[j : j + 1, :], (TILE, TILE))
+    parts = (rest[:first], fresh, rest[first + 8 :])
+    return jnp.concatenate([part for part in parts if part.shape[0]], axis=0)
+
+
+def invert_block(a):
+    for first in range(0, TILE, 8):
+        a = eliminate(a, first)
+    return a
+
+
+def invert_kernel(k_ref, o_ref):
+    o_ref[...] = k_ref[...]
+
+    def step(b, carry):
+        own = pl.ds(pl.multiple_of(b * TILE, TILE), TILE)
+        block = invert_block(o_ref[own, own])
+        rows = exact_dot(block, o_ref[own, :])
+        cols = o_ref[:, own]
+        o_ref[...] = o_ref[...] - exact_dot(cols, rows)
+        o_ref[:, own] = -exact_dot(cols, block)
+        o_ref[own, :] = rows
+        o_ref[own, own] = block
+        return carry
+
+    lax.fori_loop(0, o_ref.shape[0] // TILE, step, 0)
+
+
+def inverse_of(kmat):
+    return pl.pallas_call(
+        invert_kernel,
+        out_shape=jax.ShapeDtypeStruct(kmat.shape, F32),
+        compiler_params=pltpu.CompilerParams(vmem_limit_bytes=32 << 20),
+        name="inverse",
+    )(kmat)
+
+
 def body(
     particle_vectors,
     observed,
@@ -70,7 +135,17 @@
     exit_offsets,
 ):
     owned, local_width = particle_vectors.shape
-    stream = particle_vectors.reshape(owned * local_width // PW, PW)
+    mem_count = lax.axis_size(MEM)
+    member_total = owned * mem_count
+    state_total = local_width * lax.axis_size("rep")
+    axes = (("mem_0", "mem_1"), ("mem_2", "rep"))
+    own_states, own_observed = (
+        lax.all_to_all(particle_vectors, MEM, split_axis=1, concat_axis=0, tiled=True),
+        lax.all_to_all(observed, MEM, split_axis=1, concat_axis=0, tiled=True),
+    )
+    block_width = own_states.shape[1]
+    patches = [own_states[:, at : at + PW] for at in range(0, block_width, PW)]
+    stream = jnp.concatenate(patches, axis=0)
     for layer in range(LAYERS):
         pre = (
             jnp.dot(stream, entry_projection_matrix[layer], preferred_element_type=jnp.float32)
@@ -82,53 +157,31 @@
             + jnp.dot(hidden, exit_projection_matrix[layer], preferred_element_type=jnp.float32)
             + exit_offsets[layer]
         ).astype(jnp.bfloat16)
-    particle_outcomes = stream.reshape(owned, local_width)
-    resid = (observed.astype(jnp.float32) - particle_outcomes.astype(jnp.float32)).astype(
-        jnp.bfloat16
+    own_preds = jnp.concatenate(
+        [stream[at : at + member_total] for at in range(0, stream.shape[0], member_total)], axis=1
     )
-    resid_wide = resid.astype(jnp.float32)
-    mem_count = lax.axis_size(MEM)
-    member_total = owned * mem_count
-    state_total = local_width * lax.axis_size("rep")
-    misfit_local = jnp.sum(resid_wide * resid_wide * precision)
-    damping = (
-        one_axis_at_a_time(misfit_local, (("mem_0", "mem_1"), ("mem_2", "rep")))
-        / (member_total * state_total)
-        + 1e-06
-    )
-    own_states, own_preds, own_resid = (
-        lax.all_to_all(particle_vectors, MEM, split_axis=1, concat_axis=0, tiled=True),
-        lax.all_to_all(particle_outcomes, MEM, split_axis=1, concat_axis=0, tiled=True),
-        lax.all_to_all(resid, MEM, split_axis=1, concat_axis=0, tiled=True),
-    )
-    block_width = own_states.shape[1]
     prec_block = lax.dynamic_slice_in_dim(precision, lax.axis_index(MEM) * block_width, block_width)
     pred_wide = own_preds.astype(jnp.float32)
+    own_resid = (own_observed.astype(jnp.float32) - pred_wide).astype(jnp.bfloat16)
+    resid_wide = own_resid.astype(jnp.float32)
+    misfit = jnp.sum(resid_wide * resid_wide * prec_block)
+    damping = one_axis_at_a_time(misfit, axes) / (member_total * state_total) + 1e-06
     pred_dev = (pred_wide - jnp.mean(pred_wide, axis=0)).astype(jnp.bfloat16)
     state_wide = own_states.astype(jnp.float32)
     state_dev = (state_wide - jnp.mean(state_wide, axis=0)).astype(jnp.bfloat16)
     weighted = (pred_dev.astype(jnp.float32) * prec_block).astype(jnp.bfloat16)
     joint = sum_by_axis(
         jnp.concatenate([contract(weighted, pred_dev), contract(own_resid, weighted)], axis=1),
-        (("mem_0", "mem_1"), ("mem_2", "rep")),
+        axes,
         0,
     )
-    gram = (
-        whole_of(joint[:, :member_total], (("mem_0", "mem_1"), ("mem_2", "rep")), 0) / state_total
-    )
+    gram = whole_of(joint[:, :member_total], axes, 0) / state_total
     cross = joint[:, member_total:] / state_total
     kmat = gram + damping * jnp.eye(member_total, dtype=jnp.float32)
-    factor = jnp.linalg.cholesky(kmat)
-    middle = jax.scipy.linalg.solve_triangular(factor, cross.T, lower=True)
-    solved = jax.scipy.linalg.solve_triangular(factor, middle, lower=True, trans="T")
-    mixing = solved.T.astype(jnp.bfloat16)
+    mixing = exact_dot(cross, inverse_of(kmat)).astype(jnp.bfloat16)
     fresh = (
         state_wide
-        + jnp.dot(
-            whole_of(mixing, (("mem_0", "mem_1"), ("mem_2", "rep")), 0),
-            state_dev,
-            preferred_element_type=jnp.float32,
-        )
+        + jnp.dot(whole_of(mixing, axes, 0), state_dev, preferred_element_type=jnp.float32)
     ).astype(jnp.bfloat16)
     return lax.all_to_all(fresh, MEM, split_axis=0, concat_axis=1, tiled=True)
 

time: 415 us -> 261 us (0.63)
  the two profiles are of different devices: /device:TPU:8 before, /device:TPU:1 now
where the time goes in v1:
time: 261 us; the launch traced here: 260 us
  waiting for transfers between devices  104 us (40%)
  starting transfers between devices  60.9 us (23%)
  blocking collectives  36.4 us (14%)
  Pallas kernels  21.8 us (8%)
  local copies, waits for them, and re-layouts  19.3 us (7%)
  matrix products  8.17 us (3%)
  other arithmetic  7.79 us (3%)
    all_to_all x5, waiting for transfers between devices, copy_for_each(): return lax.all_to_all(copies, axis, split_axis=0, concat_axis=0, tiled=True)  43 us
    all_to_all x5, starting transfers between devices, copy_for_each(): return lax.all_to_all(copies, axis, split_axis=0, concat_axis=0, tiled=True)  25.4 us
    all_to_all x1, blocking collectives, body(): return lax.all_to_all(fresh, MEM, split_axis=0, concat_axis=1, tiled=True)  24 us
    all_to_all x1, waiting for transfers between devices, sent_and_summed(): lax.all_to_all(cut_along(array, dim, length), axis, 0, 0, tiled=True)  24 us
    pallas_call x1, Pallas kernels, inverse_of(): pl.pallas_call(invert_kernel, out_shape=jax.ShapeDtypeStruct(kmat.shape,...  21.8 us
    all_to_all x1, starting transfers between devices, body(): lax.all_to_all(particle_vectors, MEM, split_axis=1, concat_axis=0, tiled=...  16.5 us
    all_to_all x1, waiting for transfers between devices, body(): lax.all_to_all(particle_vectors, MEM, split_axis=1, concat_axis=0, tiled=...  16 us
    all_to_all x1, blocking collectives, copy_for_each(): return lax.all_to_all(copies, axis, split_axis=0, concat_axis=0, tiled=True)  12.4 us
  transfers between devices with their start and end apart: 9, of which 9 were waited for; matrix products, arithmetic and copies ran while one was open for 6% of the time, Pallas kernels for 0%

profile of v1, /device:TPU:1, one launch (start us, length us, event | category | flops | bytes accessed | tf_op | source)
XLA Modules:
  0.0 259.7 jit_solution(6469270974554619863)
XLA Ops:
  0.0 16.5 %all-to-all-start = ((bf16[4,128,512]{2,0,1:T(4,128)(2,1)}), bf16[4,128,512]{2,0,1:T(4,128)(2,1)S(1)}, u32[]{:S(2)}, u32[]{:S(2)}) async-start(bf16[4,128,512]{2,0,1:T(4,128)(2,1)} %bitcast.42), calls=%async_computation | async-start | bytes 1048576 | tf_op jit(solution)/shard_map/all_to_all | solution.py:143
  18.8 16.0 %all-to-all-done = bf16[4,128,512]{2,0,1:T(4,128)(2,1)S(1)} async-done(((bf16[4,128,512]{2,0,1:T(4,128)(2,1)}), bf16[4,128,512]{2,0,1:T(4,128)(2,1)S(1)}, u32[]{:S(2)}, u32[]{:S(2)}) %all-to-all-start) | async-done | bytes 524320 | tf_op jit(solution)/shard_map/all_to_all | solution.py:143
  34.8 7.1 %all-to-all-start.1 = ((bf16[4,128,512]{2,0,1:T(4,128)(2,1)}), bf16[4,128,512]{2,0,1:T(4,128)(2,1)S(1)}, u32[]{:S(2)}, u32[]{:S(2)}) async-start(bf16[4,128,512]{2,0,1:T(4,128)(2,1)} %bitcast.43), calls=%async_computation.1 | async-start | bytes 1048576 | tf_op jit(solution)/shard_map/all_to_all | solution.py:144
  42.1 3.4 %fusion.2 = bf16[1024,256]{1,0:T(8,128)(2,1)} fusion(f32[1024]{0:T(1024)S(1)} %bitcast.45, bf16[512,256]{1,0:T(8,128)(2,1)S(1)} %get-tuple-element.8, bf16[512,256]{1,0:T(8,128)(2,1)S(1)} %get-tuple-element.7, f32[256]{0:T(256)S(1)} %bitcast.47, bf16[2,1024,256]{2,1,0:T(8,128)(2,1)S(1)} %copy-done.3, bf16[2,256,1024]{2,1,0:T(8,128)(2,1)} %param.10), kind=kOutput, calls=%fused_computation.13 | convolution fusion | flops 1082916864 | bytes 2626560 | tf_op jit(solution)/shard_map/dot_general | solution.py:157
  45.4 2.8 %fusion.3 = bf16[1024,256]{1,0:T(8,128)(2,1)S(1)} fusion(bf16[1024,256]{1,0:T(8,128)(2,1)} %fusion.2, f32[1024]{0:T(1024)S(1)} %bitcast.44, f32[256]{0:T(256)S(1)} %bitcast.46, bf16[2,1024,256]{2,1,0:T(8,128)(2,1)S(1)} %copy-done.3, bf16[2,256,1024]{2,1,0:T(8,128)(2,1)} %param.10), kind=kOutput, calls=%fused_computation.14 | convolution fusion | flops 1081081856 | bytes 2626560 | tf_op jit(solution)/shard_map/dot_general | solution.py:157
  48.4 10.5 %all-to-all-done.1 = bf16[4,128,512]{2,0,1:T(4,128)(2,1)S(1)} async-done(((bf16[4,128,512]{2,0,1:T(4,128)(2,1)}), bf16[4,128,512]{2,0,1:T(4,128)(2,1)S(1)}, u32[]{:S(2)}, u32[]{:S(2)}) %all-to-all-start.1) | async-done | bytes 524320 | tf_op jit(solution)/shard_map/all_to_all | solution.py:144
  64.7 2.5 reshape_reshape.7
  69.4 8.0 %all-to-all-start.2 = ((f32[8,32,2,1024]{3,2,1,0:T(2,128)}), f32[8,32,2,1024]{3,2,1,0:T(2,128)S(1)}, u32[]{:S(2)}, u32[]{:S(2)}) async-start(f32[8,32,2,1024]{3,2,1,0:T(2,128)} %copy.32), calls=%async_computation.2 | async-start | bytes 4194304 | tf_op jit(solution)/shard_map/all_to_all | solution.py:36
  79.9 24.0 %all-to-all-done.2 = f32[8,32,2,1024]{3,2,1,0:T(2,128)S(1)} async-done(((f32[8,32,2,1024]{3,2,1,0:T(2,128)}), f32[8,32,2,1024]{3,2,1,0:T(2,128)S(1)}, u32[]{:S(2)}, u32[]{:S(2)}) %all-to-all-start.2) | async-done | bytes 2097184 | tf_op jit(solution)/shard_map/all_to_all | solution.py:36
  105.0 4.0 %all-to-all-start.6 = ((f32[8,1,1]{2,1,0:T(1,128)}), f32[8,1,1]{2,1,0:T(1,128)S(1)}, u32[]{:S(2)}, u32[]{:S(2)}) async-start(f32[8,1,1]{2,1,0:T(1,128)} %broadcast_in_dim.24), calls=%async_computation.6 | async-start | bytes 8192 | tf_op jit(solution)/shard_map/all_to_all | solution.py:16
  110.7 3.0 %all-to-all-done.6 = f32[8,1,1]{2,1,0:T(1,128)S(1)} async-done(((f32[8,1,1]{2,1,0:T(1,128)}), f32[8,1,1]{2,1,0:T(1,128)S(1)}, u32[]{:S(2)}, u32[]{:S(2)}) %all-to-all-start.6) | async-done | bytes 64 | tf_op jit(solution)/shard_map/all_to_all | solution.py:16
  113.7 3.9 %all-to-all-start.3 = ((f32[32,2,1024]{2,1,0:T(2,128)}), f32[32,2,1024]{2,1,0:T(2,128)S(1)}, u32[]{:S(2)}, u32[]{:S(2)}) async-start(f32[32,2,1024]{2,1,0:T(2,128)} %reduce_sum.64), calls=%async_computation.3 | async-start | bytes 524288 | tf_op jit(solution)/shard_map/all_to_all | solution.py:43
  118.1 10.9 %all-to-all-done.3 = f32[32,2,1024]{2,1,0:T(2,128)S(1)} async-done(((f32[32,2,1024]{2,1,0:T(2,128)}), f32[32,2,1024]{2,1,0:T(2,128)S(1)}, u32[]{:S(2)}, u32[]{:S(2)}) %all-to-all-start.3) | async-done | bytes 262176 | tf_op jit(solution)/shard_map/all_to_all | solution.py:43
  130.2 4.5 %all-to-all-start.7 = ((f32[32,1,1]{2,1,0:T(1,128)}), f32[32,1,1]{2,1,0:T(1,128)S(1)}, u32[]{:S(2)}, u32[]{:S(2)}) async-start(f32[32,1,1]{2,1,0:T(1,128)} %broadcast_in_dim.25), calls=%async_computation.7 | async-start | bytes 32768 | tf_op jit(solution)/shard_map/all_to_all | solution.py:16
  134.8 8.4 %all-to-all-done.7 = f32[32,1,1]{2,1,0:T(1,128)S(1)} async-done(((f32[32,1,1]{2,1,0:T(1,128)}), f32[32,1,1]{2,1,0:T(1,128)S(1)}, u32[]{:S(2)}, u32[]{:S(2)}) %all-to-all-start.7) | async-done | bytes 160 | tf_op jit(solution)/shard_map/all_to_all | solution.py:16
  143.3 12.4 %all_to_all.93 = f32[32,2,512]{2,1,0:T(2,128)S(1)} all-to-all(f32[32,2,512]{2,1,0:T(2,128)S(1)} %broadcast_in_dim.22), channel_id=1, replica_groups=mesh['mem_0'=8,'mem_1'=4,'mem_2'=4,'rep'=2] {'mem_0','mem_1'}, dimensions={0} | all-to-all | bytes 262144 | tf_op jit(solution)/shard_map/all_to_all | solution.py:16
  156.9 7.6 %all-to-all-start.5 = ((f32[8,32,2,512]{3,2,1,0:T(2,128)}), f32[8,32,2,512]{3,2,1,0:T(2,128)S(1)}, u32[]{:S(2)}, u32[]{:S(2)}) async-start(f32[8,32,2,512]{3,2,1,0:T(2,128)} %broadcast_in_dim.23), calls=%async_computation.5 | async-start | bytes 2097152 | tf_op jit(solution)/shard_map/all_to_all | solution.py:16
  165.8 13.8 %all-to-all-done.5 = f32[8,32,2,512]{3,2,1,0:T(2,128)S(1)} async-done(((f32[8,32,2,512]{3,2,1,0:T(2,128)}), f32[8,32,2,512]{3,2,1,0:T(2,128)S(1)}, u32[]{:S(2)}, u32[]{:S(2)}) %all-to-all-start.5) | async-done | bytes 1048608 | tf_op jit(solution)/shard_map/all_to_all | solution.py:16
  181.6 21.8 %inverse.1 = f32[512,512]{1,0:T(8,128)S(1)} custom-call(f32[512,512]{1,0:T(8,128)S(1)} %select_add_fusion.k_ref), custom_call_target="tpu_custom_call" | custom-call | tf_op jit(solution)/shard_map/inverse/pallas_call | solution.py:120
  204.8 3.9 %all-to-all-start.8 = ((bf16[32,2,512]{2,1,0:T(2,128)(2,1)}), bf16[32,2,512]{2,1,0:T(2,128)(2,1)S(1)}, u32[]{:S(2)}, u32[]{:S(2)}) async-start(bf16[32,2,512]{2,1,0:T(2,128)(2,1)} %broadcast_in_dim.26), calls=%async_computation.8 | async-start | bytes 131072 | tf_op jit(solution)/shard_map/all_to_all | solution.py:16
  208.9 8.6 %all-to-all-done.8 = bf16[32,2,512]{2,1,0:T(2,128)(2,1)S(1)} async-done(((bf16[32,2,512]{2,1,0:T(2,128)(2,1)}), bf16[32,2,512]{2,1,0:T(2,128)(2,1)S(1)}, u32[]{:S(2)}, u32[]{:S(2)}) %all-to-all-start.8) | async-done | bytes 65568 | tf_op jit(solution)/shard_map/all_to_all | solution.py:16
  218.6 5.4 %all-to-all-start.9 = ((bf16[8,32,2,512]{3,2,1,0:T(2,128)(2,1)}), bf16[8,32,2,512]{3,2,1,0:T(2,128)(2,1)S(1)}, u32[]{:S(2)}, u32[]{:S(2)}) async-start(bf16[8,32,2,512]{3,2,1,0:T(2,128)(2,1)} %broadcast_in_dim.27), calls=%async_computation.9 | async-start | bytes 1048576 | tf_op jit(solution)/shard_map/all_to_all | solution.py:16
  224.3 9.1 %all-to-all-done.9 = bf16[8,32,2,512]{3,2,1,0:T(2,128)(2,1)S(1)} async-done(((bf16[8,32,2,512]{3,2,1,0:T(2,128)(2,1)}), bf16[8,32,2,512]{3,2,1,0:T(2,128)(2,1)S(1)}, u32[]{:S(2)}, u32[]{:S(2)}) %all-to-all-start.9) | async-done | bytes 524320 | tf_op jit(solution)/shard_map/all_to_all | solution.py:16
  234.8 24.0 %all_to_all.94 = bf16[128,4,512]{2,1,0:T(4,128)(2,1)S(1)} all-to-all(bf16[128,4,512]{2,1,0:T(4,128)(2,1)S(1)} %all_to_all.78), channel_id=1, replica_groups=mesh['mem_0'=8,'mem_1'=4,'mem_2'=4,'rep'=2] {'mem_0','mem_1','mem_2'}, dimensions={0} | all-to-all | bytes 1048576 | tf_op jit(solution)/shard_map/all_to_all | solution.py:186
  (51 shorter events, 26.6 us)
Async XLA Ops:
  0.0 42.0 %copy-start.3 = (bf16[2,1024,256]{2,1,0:T(8,128)(2,1)S(1)}, bf16[2,1024,256]{2,1,0:T(8,128)(2,1)}, u32[]{:S(2)}) copy-start(bf16[2,1024,256]{2,1,0:T(8,128)(2,1)} %param.12) | copy-start | bytes 3145732
  0.0 34.8 %all-to-all-start = ((bf16[4,128,512]{2,0,1:T(4,128)(2,1)}), bf16[4,128,512]{2,0,1:T(4,128)(2,1)S(1)}, u32[]{:S(2)}, u32[]{:S(2)}) async-start(bf16[4,128,512]{2,0,1:T(4,128)(2,1)} %bitcast.42), calls=%async_computation | async-start | bytes 1048576 | tf_op jit(solution)/shard_map/all_to_all | solution.py:143
  34.8 24.2 %all-to-all-start.1 = ((bf16[4,128,512]{2,0,1:T(4,128)(2,1)}), bf16[4,128,512]{2,0,1:T(4,128)(2,1)S(1)}, u32[]{:S(2)}, u32[]{:S(2)}) async-start(bf16[4,128,512]{2,0,1:T(4,128)(2,1)} %bitcast.43), calls=%async_computation.1 | async-start | bytes 1048576 | tf_op jit(solution)/shard_map/all_to_all | solution.py:144
  42.0 3.5 %copy-start.1 = (bf16[512,512]{1,0:T(8,128)(2,1)}, bf16[512,512]{1,0:T(8,128)(2,1)S(1)}, u32[]{:S(2)}) copy-start(bf16[512,512]{1,0:T(8,128)(2,1)S(1)} %all_to_all.67) | copy-start | bytes 1572868
  58.9 3.2 %copy-start = (bf16[4,128,512]{2,0,1:T(4,128)(2,1)}, bf16[4,128,512]{2,0,1:T(4,128)(2,1)S(1)}, u32[]{:S(2)}) copy-start(bf16[4,128,512]{2,0,1:T(4,128)(2,1)S(1)} %all-to-all-done.1) | copy-start | bytes 1572868
  69.4 34.4 %all-to-all-start.2 = ((f32[8,32,2,1024]{3,2,1,0:T(2,128)}), f32[8,32,2,1024]{3,2,1,0:T(2,128)S(1)}, u32[]{:S(2)}, u32[]{:S(2)}) async-start(f32[8,32,2,1024]{3,2,1,0:T(2,128)} %copy.32), calls=%async_computation.2 | async-start | bytes 4194304 | tf_op jit(solution)/shard_map/all_to_all | solution.py:36
  105.0 8.6 %all-to-all-start.6 = ((f32[8,1,1]{2,1,0:T(1,128)}), f32[8,1,1]{2,1,0:T(1,128)S(1)}, u32[]{:S(2)}, u32[]{:S(2)}) async-start(f32[8,1,1]{2,1,0:T(1,128)} %broadcast_in_dim.24), calls=%async_computation.6 | async-start | bytes 8192 | tf_op jit(solution)/shard_map/all_to_all | solution.py:16
  113.7 15.4 %all-to-all-start.3 = ((f32[32,2,1024]{2,1,0:T(2,128)}), f32[32,2,1024]{2,1,0:T(2,128)S(1)}, u32[]{:S(2)}, u32[]{:S(2)}) async-start(f32[32,2,1024]{2,1,0:T(2,128)} %reduce_sum.64), calls=%async_computation.3 | async-start | bytes 524288 | tf_op jit(solution)/shard_map/all_to_all | solution.py:43
  130.2 13.0 %all-to-all-start.7 = ((f32[32,1,1]{2,1,0:T(1,128)}), f32[32,1,1]{2,1,0:T(1,128)S(1)}, u32[]{:S(2)}, u32[]{:S(2)}) async-start(f32[32,1,1]{2,1,0:T(1,128)} %broadcast_in_dim.25), calls=%async_computation.7 | async-start | bytes 32768 | tf_op jit(solution)/shard_map/all_to_all | solution.py:16
  156.9 22.7 %all-to-all-start.5 = ((f32[8,32,2,512]{3,2,1,0:T(2,128)}), f32[8,32,2,512]{3,2,1,0:T(2,128)S(1)}, u32[]{:S(2)}, u32[]{:S(2)}) async-start(f32[8,32,2,512]{3,2,1,0:T(2,128)} %broadcast_in_dim.23), calls=%async_computation.5 | async-start | bytes 2097152 | tf_op jit(solution)/shard_map/all_to_all | solution.py:16
  204.8 12.7 %all-to-all-start.8 = ((bf16[32,2,512]{2,1,0:T(2,128)(2,1)}), bf16[32,2,512]{2,1,0:T(2,128)(2,1)S(1)}, u32[]{:S(2)}, u32[]{:S(2)}) async-start(bf16[32,2,512]{2,1,0:T(2,128)(2,1)} %broadcast_in_dim.26), calls=%async_computation.8 | async-start | bytes 131072 | tf_op jit(solution)/shard_map/all_to_all | solution.py:16
  218.6 14.9 %all-to-all-start.9 = ((bf16[8,32,2,512]{3,2,1,0:T(2,128)(2,1)}), bf16[8,32,2,512]{3,2,1,0:T(2,128)(2,1)S(1)}, u32[]{:S(2)}, u32[]{:S(2)}) async-start(bf16[8,32,2,512]{3,2,1,0:T(2,128)(2,1)} %broadcast_in_dim.27), calls=%async_computation.9 | async-start | bytes 1048576 | tf_op jit(solution)/shard_map/all_to_all | solution.py:16
  224.0 10.3 %copy-start.2 = (bf16[512,512]{1,0:T(8,128)(2,1)S(1)}, bf16[512,512]{1,0:T(8,128)(2,1)}, u32[]{:S(2)}) copy-start(bf16[512,512]{1,0:T(8,128)(2,1)} %copy-done.1) | copy-start | bytes 1572868

commit v2 on v1

v2 whole, which is shorter than its diff:
```python
import functools

import jax
import jax.numpy as jnp
from jax import lax
from jax.experimental import pallas as pl
from jax.experimental.pallas import tpu as pltpu
from jax.sharding import PartitionSpec as P

F32 = jnp.float32
BF16 = jnp.bfloat16
MESH = pl.DeviceIdType.MESH
PW = 256
LAYERS = 2
TILE = 128
NZ, NY, NX = 8, 4, 4
PLANE = NY * NX
PEERS = NZ * PLANE
CORES = 2
MEMBERS = 512
STATE = 131072
OWNED = MEMBERS // PEERS
BLOCK = STATE // CORES // PEERS
TILES = MEMBERS // TILE
LOWER = [(i, j) for i in range(TILES) for j in range(i + 1)]
GRAM_ROWS = len(LOWER) * TILE // CORES // PLANE
CROSS_ROWS = MEMBERS // CORES // PLANE
CHUNK = 256
GROUPS = CHUNK // OWNED


def exact_dot(left, right):
    return jnp.dot(left, right, precision=lax.Precision.HIGHEST, preferred_element_type=F32)


def contract(left, right):
    return lax.dot_general(left, right, (((1,), (1,)), ((), ())), preferred_element_type=F32)


def eliminate(a, first):
    sub = lax.broadcasted_iota(jnp.int32, (8, TILE), 0)
    lane = lax.broadcasted_iota(jnp.int32, (8, TILE), 1)
    rows = a[first : first + 8, :]
    own = (lane >= first) & (lane < first + 8)
    fresh = jnp.where(own, jnp.where(lane - first == sub, 1.0, 0.0), rows)
    cols = [jnp.broadcast_to(rows[:, first + j : first + j + 1], (8, TILE)) for j in range(8)]
    for k in range(8):
        inverse = 1.0 / jnp.broadcast_to(cols[k][k : k + 1, :], (8, TILE))
        row = jnp.broadcast_to(fresh[k : k + 1, :], (8, TILE)) * inverse
        fresh = jnp.where(sub == k, row, fresh - cols[k] * row)
        for j in range(k + 1, 8):
            entry = jnp.broadcast_to(cols[j][k : k + 1, :], (8, TILE)) * inverse
            cols[j] = jnp.where(sub == k, entry, cols[j] - cols[k] * entry)
    lanes = lax.broadcasted_iota(jnp.int32, (TILE, TILE), 1)
    rest = jnp.where((lanes >= first) & (lanes < first + 8), 0.0, a)
    for j in range(8):
        left = jnp.broadcast_to(a[:, first + j : first + j + 1], (TILE, TILE))
        rest = rest - left * jnp.broadcast_to(fresh[j : j + 1, :], (TILE, TILE))
    parts = (rest[:first], fresh, rest[first + 8 :])
    return jnp.concatenate([part for part in parts if part.shape[0]], axis=0)


def invert_block(a):
    for first in range(0, TILE, 8):
        a = eliminate(a, first)
    return a


def invert_step(k_ref, b):
    own = slice(b * TILE, (b + 1) * TILE)
    block = invert_block(k_ref[own, own])
    rows = exact_dot(block, k_ref[own, :])
    cols = k_ref[:, own]
    k_ref[...] = k_ref[...] - exact_dot(cols, rows)
    k_ref[:, own] = -exact_dot(cols, block)
    k_ref[own, :] = rows
    k_ref[own, own] = block


def forecast(x, up_ref, up_bias_ref, down_ref, down_bias_ref):
    for layer in range(LAYERS):
        half = 0.5 * (
            jnp.dot(x, up_ref[layer], preferred_element_type=F32) + up_bias_ref[layer : layer + 1, :]
        )
        hidden = (half + half * jnp.tanh(half)).astype(BF16)
        x = (
            x.astype(F32)
            + jnp.dot(hidden, down_ref[layer], preferred_element_type=F32)
            + down_bias_ref[layer : layer + 1, :]
        ).astype(BF16)
    return x


def wait_for(ref, sem):
    pltpu.make_async_copy(ref, ref, sem).wait()


def kernel(
    x_hbm, obs_hbm, prec_hbm, up_hbm, up_bias, down_hbm, down_bias, out_ref,
    x_own, obs_own, prec_in, prec, up, down, x_in, obs_in, pred, states, dev, weighted, back,
    gram, gram_pair, gram_half, gram_plane, gram_z, gram_all,
    cross, cross_pair, cross_half, cross_plane, cross_z, cross_all, kmat,
    load_sem, own_sem, send_sem, recv_sem,
):
    me, core = lax.axis_index("mem"), lax.axis_index("rep")
    z, q = me // PLANE, lax.rem(me, PLANE)
    y, x = q // NX, lax.rem(q, NX)

    loads = [
        pltpu.make_async_copy(src, dst, load_sem.at[i])
        for i, (src, dst) in enumerate(
            [(up_hbm, up), (down_hbm, down), (prec_hbm, prec_in), (x_hbm, x_own), (obs_hbm, obs_own)]
        )
    ]
    own_copies = [
        pltpu.make_async_copy(x_hbm.at[me], x_in.at[me], own_sem.at[0]),
        pltpu.make_async_copy(obs_hbm.at[me], obs_in.at[me], own_sem.at[1]),
    ]

    def plane_peer(s):
        return lax.rem(y + s // NX, NY) * NX + lax.rem(x + lax.rem(s, NX), NX)

    def peer(s):
        return lax.rem(z + lax.rem(s, NZ), NZ) * PLANE + plane_peer(s // NZ)

    barrier = pltpu.get_barrier_semaphore()

    def greet(s, carry):
        pl.semaphore_signal(barrier, 1, device_id={"mem": peer(s)}, device_id_type=MESH)
        return carry

    pl.semaphore_signal(barrier, 1, device_id={"rep": 1 - core}, device_id_type=MESH)
    lax.fori_loop(1, PEERS, greet, 0)
    for copy in own_copies + loads:
        copy.start()
    pl.semaphore_wait(barrier, PEERS)

    def send(src, dst, i, target):
        pltpu.make_async_remote_copy(
            src_ref=src, dst_ref=dst, send_sem=send_sem.at[i], recv_sem=recv_sem.at[i],
            device_id=target, device_id_type=MESH,
        ).start()

    def exchange(src, dst, i):
        def one(s, carry):
            target = peer(s)
            send(src.at[target], dst.at[me], i, {"mem": target})
            return carry

        lax.fori_loop(1, PEERS, one, 0)

    def to_plane(src_of, dst, i):
        def one(s, carry):
            target = plane_peer(s)
            send(src_of(target), dst, i, {"mem": z * PLANE + target})
            return carry

        lax.fori_loop(1, PLANE, one, 0)

    def to_column(src, dst, i):
        def one(s, carry):
            send(src, dst, i, {"mem": lax.rem(z + s, NZ) * PLANE + q})
            return carry

        lax.fori_loop(1, NZ, one, 0)

    def sum_plane(ref, own_part):
        ref[q] = own_part
        total = ref[0]
        for s in range(1, ref.shape[0]):
            total = total + ref[s]
        return total

    others = pl.ds(0, PEERS - 1)
    exchange(x_hbm, x_in, 0)
    exchange(obs_hbm, obs_in, 1)

    for copy in loads:
        copy.wait()
    for c in range(BLOCK // TILE):
        prec[:, c * TILE : (c + 1) * TILE] = prec_in[pl.ds(c, PEERS, stride=BLOCK // TILE), :]

    def misfit_of(c, total):
        at = pl.ds(pl.multiple_of(c * GROUPS, GROUPS), GROUPS)
        rows = x_own[at].reshape(CHUNK, BLOCK)
        seen = obs_own[at].reshape(CHUNK, BLOCK)
        for p in range(0, BLOCK, PW):
            said = forecast(rows[:, p : p + PW], up, up_bias, down, down_bias)
            resid = (seen[:, p : p + PW].astype(F32) - said.astype(F32)).astype(BF16).astype(F32)
            square = (resid * resid).reshape(GROUPS, OWNED, PW).sum(axis=1)
            total = total + square * prec[at, p : p + PW]
        return total

    misfit = jnp.sum(
        lax.fori_loop(0, MEMBERS // CHUNK, misfit_of, jnp.zeros((GROUPS, PW), F32))
    ) / (MEMBERS * STATE)

    own_copies[0].wait()
    wait_for(x_in.at[others], recv_sem.at[0])

    def forecast_block(c, carry):
        rows = x_in[pl.ds(pl.multiple_of(c * GROUPS, GROUPS), GROUPS)].reshape(CHUNK, BLOCK)
        at = pl.ds(pl.multiple_of(c * CHUNK, CHUNK), CHUNK)
        states[at, :] = rows
        for p in range(0, BLOCK, PW):
            pred[at, p : p + PW] = forecast(rows[:, p : p + PW], up, up_bias, down, down_bias)
        return carry

    lax.fori_loop(0, MEMBERS // CHUNK, forecast_block, 0)
    prec_row = prec[pl.ds(me, 1), :]
    wide = pred[...].astype(F32)
    dev[...] = (wide - jnp.mean(wide, axis=0, keepdims=True)).astype(BF16)
    weighted[...] = (dev[...].astype(F32) * prec_row).astype(BF16)
    eye = lax.broadcasted_iota(jnp.int32, (TILE, TILE), 0) == lax.broadcasted_iota(
        jnp.int32, (TILE, TILE), 1
    )
    for i in range(TILES):
        rows = contract(weighted[i * TILE : (i + 1) * TILE, :], dev[: (i + 1) * TILE, :]) / STATE
        for j in range(i + 1):
            part = rows[:, j * TILE : (j + 1) * TILE]
            if i == j:
                part = part + jnp.where(eye, misfit, 0.0)
            at = LOWER.index((i, j)) * TILE
            gram[at : at + TILE, :] = part

    half = GRAM_ROWS * PLANE
    theirs = pl.ds(pl.multiple_of((1 - core) * half, 8), half)
    send(gram.at[theirs], gram_pair, 2, {"rep": 1 - core})
    wide = states[...].astype(F32)
    dev[...] = (wide - jnp.mean(wide, axis=0, keepdims=True)).astype(BF16)
    wait_for(gram_pair, recv_sem.at[2])
    mine = pl.ds(pl.multiple_of(core * half, 8), half)
    gram_half[...] = (gram[mine, :] + gram_pair[...]).reshape(PLANE, GRAM_ROWS, TILE)
    to_plane(lambda target: gram_half.at[target], gram_plane.at[q], 3)
    wait_for(gram_plane.at[pl.ds(0, PLANE - 1)], recv_sem.at[3])
    gram_z[z] = sum_plane(gram_plane, gram_half[q])
    to_column(gram_z.at[z], gram_z.at[z], 4)
    wait_for(gram_z.at[pl.ds(0, NZ - 1)], recv_sem.at[4])
    total = gram_z[0]
    for s in range(1, NZ):
        total = total + gram_z[s]
    gram_all[core * PLANE + q] = total
    to_plane(lambda target: gram_all.at[core * PLANE + q], gram_all.at[core * PLANE + q], 5)

    own_copies[1].wait()
    wait_for(obs_in.at[others], recv_sem.at[1])
    for c in range(MEMBERS // CHUNK):
        at = slice(c * CHUNK, (c + 1) * CHUNK)
        seen = obs_in[c * GROUPS : (c + 1) * GROUPS].reshape(CHUNK, BLOCK)
        resid = (seen.astype(F32) - pred[at, :].astype(F32)).astype(BF16)
        cross[c] = contract(resid, weighted[...]) / STATE
    send(cross.at[1 - core], cross_pair, 7, {"rep": 1 - core})

    wait_for(gram_all.at[pl.ds(0, PLANE - 1)], recv_sem.at[5])
    summed = pl.ds(pl.multiple_of(core * PLANE, PLANE), PLANE)
    send(gram_all.at[summed], gram_all.at[summed], 6, {"rep": 1 - core})
    wait_for(cross_pair, recv_sem.at[7])
    cross_half[...] = (cross[core] + cross_pair[...]).reshape(PLANE, CROSS_ROWS, MEMBERS)
    to_plane(lambda target: cross_half.at[target], cross_plane.at[q], 8)
    wait_for(gram_all.at[summed], recv_sem.at[6])
    lower = gram_all[...].reshape(len(LOWER) * TILE, TILE)
    below = lax.broadcasted_iota(jnp.int32, (TILE, TILE), 0) >= lax.broadcasted_iota(
        jnp.int32, (TILE, TILE), 1
    )
    for n, (i, j) in enumerate(LOWER):
        part = lower[n * TILE : (n + 1) * TILE, :]
        rows, cols = slice(i * TILE, (i + 1) * TILE), slice(j * TILE, (j + 1) * TILE)
        if i == j:
            kmat[rows, cols] = jnp.where(below, part, part.T) + jnp.where(eye, 1e-06, 0.0)
        else:
            kmat[rows, cols] = part
            kmat[cols, rows] = part.T

    invert_step(kmat, 0)
    wait_for(cross_plane.at[pl.ds(0, PLANE - 1)], recv_sem.at[8])
    cross_z[z] = sum_plane(cross_plane, cross_half[q])
    to_column(cross_z.at[z], cross_z.at[z], 9)
    invert_step(kmat, 1)
    wait_for(cross_z.at[pl.ds(0, NZ - 1)], recv_sem.at[9])
    total = cross_z[0]
    for s in range(1, NZ):
        total = total + cross_z[s]
    cross_all[core * PLANE + q] = total
    to_plane(lambda target: cross_all.at[core * PLANE + q], cross_all.at[core * PLANE + q], 10)
    invert_step(kmat, 2)
    wait_for(cross_all.at[pl.ds(0, PLANE - 1)], recv_sem.at[10])
    send(cross_all.at[summed], cross_all.at[summed], 11, {"rep": 1 - core})
    invert_step(kmat, 3)
    wait_for(cross_all.at[summed], recv_sem.at[11])

    mixing = exact_dot(cross_all[...].reshape(MEMBERS, MEMBERS), kmat[...]).astype(BF16)
    for c in range(MEMBERS // CHUNK):
        at = slice(c * CHUNK, (c + 1) * CHUNK)
        moved = jnp.dot(mixing[at, :], dev[...], preferred_element_type=F32)
        fresh = (states[at, :].astype(F32) + moved).astype(BF16)
        back[c * GROUPS : (c + 1) * GROUPS] = fresh.reshape(GROUPS, OWNED, BLOCK)
    home = pltpu.make_async_copy(back.at[me], out_ref.at[me], own_sem.at[2])
    home.start()
    exchange(back, out_ref, 12)
    home.wait()

    wait_for(x_hbm.at[others], send_sem.at[0])
    wait_for(obs_hbm.at[others], send_sem.at[1])
    wait_for(gram_pair, send_sem.at[2])
    wait_for(gram_plane.at[pl.ds(0, PLANE - 1)], send_sem.at[3])
    wait_for(gram_z.at[pl.ds(0, NZ - 1)], send_sem.at[4])
    wait_for(gram_all.at[pl.ds(0, PLANE - 1)], send_sem.at[5])
    wait_for(gram_all.at[summed], send_sem.at[6])
    wait_for(cross_pair, send_sem.at[7])
    wait_for(cross_plane.at[pl.ds(0, PLANE - 1)], send_sem.at[8])
    wait_for(cross_z.at[pl.ds(0, NZ - 1)], send_sem.at[9])
    wait_for(cross_all.at[pl.ds(0, PLANE - 1)], send_sem.at[10])
    wait_for(cross_all.at[summed], send_sem.at[11])
    wait_for(back.at[others], send_sem.at[12])
    wait_for(out_ref.at[others], recv_sem.at[12])


def body(states, observed, precision, up, up_bias, down, down_bias):
    def by_block(array):
        return array.reshape(OWNED, PEERS, BLOCK).transpose(1, 0, 2)

    anywhere = pl.BlockSpec(memory_space=pl.ANY)
    vmem = pl.BlockSpec(memory_space=pltpu.VMEM)
    slabs = (PEERS, OWNED, BLOCK)
    square = (MEMBERS, BLOCK)
    out = pl.pallas_call(
        kernel,
        out_shape=jax.ShapeDtypeStruct(slabs, BF16),
        in_specs=[anywhere, anywhere, anywhere, anywhere, vmem, anywhere, vmem],
        out_specs=anywhere,
        scratch_shapes=[
            pltpu.VMEM(slabs, BF16),
            pltpu.VMEM(slabs, BF16),
            pltpu.VMEM((PEERS * BLOCK // TILE, TILE), F32),
            pltpu.VMEM((PEERS, BLOCK), F32),
            pltpu.VMEM(up.shape, BF16),
            pltpu.VMEM(down.shape, BF16),
            pltpu.VMEM(slabs, BF16),
            pltpu.VMEM(slabs, BF16),
            pltpu.VMEM(square, BF16),
            pltpu.VMEM(square, BF16),
            pltpu.VMEM(square, BF16),
            pltpu.VMEM(square, BF16),
            pltpu.VMEM(slabs, BF16),
            pltpu.VMEM((len(LOWER) * TILE, TILE), F32),
            pltpu.VMEM((GRAM_ROWS * PLANE, TILE), F32),
            pltpu.VMEM((PLANE, GRAM_ROWS, TILE), F32),
            pltpu.VMEM((PLANE, GRAM_ROWS, TILE), F32),
            pltpu.VMEM((NZ, GRAM_ROWS, TILE), F32),
            pltpu.VMEM((CORES * PLANE, GRAM_ROWS, TILE), F32),
            pltpu.VMEM((CORES, MEMBERS // CORES, MEMBERS), F32),
            pltpu.VMEM((MEMBERS // CORES, MEMBERS), F32),
            pltpu.VMEM((PLANE, CROSS_ROWS, MEMBERS), F32),
            pltpu.VMEM((PLANE, CROSS_ROWS, MEMBERS), F32),
            pltpu.VMEM((NZ, CROSS_ROWS, MEMBERS), F32),
            pltpu.VMEM((CORES * PLANE, CROSS_ROWS, MEMBERS), F32),
            pltpu.VMEM((MEMBERS, MEMBERS), F32),
            pltpu.SemaphoreType.DMA((5,)),
            pltpu.SemaphoreType.DMA((3,)),
            pltpu.SemaphoreType.DMA((13,)),
            pltpu.SemaphoreType.DMA((13,)),
        ],
        compiler_params=pltpu.CompilerParams(
            collective_id=0, has_side_effects=True, vmem_limit_bytes=56 << 20
        ),
        name="ensemble_update",
    )(
        by_block(states),
        by_block(observed),
        precision.reshape(PEERS * BLOCK // TILE, TILE),
        up,
        up_bias,
        down,
        down_bias,
    )
    return out.transpose(1, 0, 2).reshape(OWNED, PEERS * BLOCK)


def solution(mesh):
    return jax.shard_map(
        body,
        mesh=mesh,
        in_specs=(P("mem", "rep"), P("mem", "rep"), P("rep"), P(), P(), P(), P()),
        out_specs=P("mem", "rep"),
        check_vma=False,
    )
```

time: 261 us -> 108 us (0.41)
  waiting for transfers between devices: 104 us -> 0 us
  Pallas kernels: 21.8 us -> 106 us
  starting transfers between devices: 60.9 us -> 0 us
  blocking collectives: 36.4 us -> 0 us
  local copies, waits for them, and re-layouts: 19.3 us -> 2.02 us
  matrix products: 8.17 us -> 0 us
  other arithmetic: 7.79 us -> 0 us
    all_to_all x9 -> x0, waiting for transfers between devices: 104 us -> none  [the longest x5 43 us: copy_for_each(): return lax.all_to_all(copies, axis, split_axis=0, concat_axis=0, tiled=True)]
    pallas_call x1, Pallas kernels: 21.8 us -> 106 us  [body(): pl.pallas_call(kernel, out_shape=jax.ShapeDtypeStruct(slabs, BF16), in_sp...]
    all_to_all x9 -> x0, starting transfers between devices: 60.9 us -> none  [the longest x5 25.4 us: copy_for_each(): return lax.all_to_all(copies, axis, split_axis=0, concat_axis=0, tiled=True)]
    all_to_all x2 -> x0, blocking collectives: 36.4 us -> none  [the longest x1 24 us: body(): return lax.all_to_all(fresh, MEM, split_axis=0, concat_axis=1, tiled=True)]
    dot_general x6 -> x0, matrix products: 8.17 us -> none  [the longest x2 6.16 us: body(): jnp.dot(hidden, exit_projection_matrix[layer], preferred_element_type=jnp...]
    reduce_sum x7 -> x0, other arithmetic: 5.61 us -> none  [the longest x1 2.26 us: body(): misfit = jnp.sum(resid_wide * resid_wide * prec_block)]
    broadcast_in_dim x6 -> x0, local copies, waits for them, and re-layouts: 5.41 us -> none  [copy_for_each(): copies = jnp.broadcast_to(array, (lax.axis_size(axis), *array.shape))]
    transpose x2 -> x0, local copies, waits for them, and re-layouts: 2.76 us -> none  [the longest x1 2.22 us: cut_along(): return jnp.moveaxis(pieces, dim, 0)]
  transfers between devices with their start and end apart: 9 -> 0, of which waited for: 9 -> 0; matrix products, arithmetic and copies ran while one was open for 6% -> 0% of each run, Pallas kernels for 0% -> 0%
where the time goes in v2:
time: 108 us
  Pallas kernels  106 us (98%)
  local copies, waits for them, and re-layouts  2.02 us (2%)
    pallas_call x1, Pallas kernels, body(): pl.pallas_call(kernel, out_shape=jax.ShapeDtypeStruct(slabs, BF16), in_sp...  106 us

profile of v2, /device:TPU:1, one launch (start us, length us, event | category | flops | bytes accessed | tf_op | source)
XLA Modules:
  0.0 107.9 jit_solution(18141328509751800561)
XLA Ops:
  0.0 105.9 %ensemble_update.1 = bf16[128,4,512]{2,1,0:T(4,128)(2,1)} custom-call(bf16[128,4,512]{2,1,0:T(4,128)(2,1)} %bitcast.11, bf16[128,4,512]{2,1,0:T(4,128)(2,1)} %bitcast.12, f32[512,128]{1,0:T(8,128)} %bitcast.13, bf16[2,256,1024]{2,1,0:T(8,128)(2,1)} %up_hbm.1, f32[2,1024]{1,0:T(2,128)} %up_bias.1, bf16[2,1024,256]{2,1,0:T(8,128)(2,1)} %down_hbm.1, ...), custom_call_target="tpu_custom_call" | custom-call | tf_op jit(solution)/shard_map/ensemble_update/pallas_call | solution.py:326
  105.9 2.0 %copy.9 = bf16[4,65536]{1,0:T(4,128)(2,1)} copy(bf16[4,65536]{1,0:T(4,128)(2,1)} %bitcast.10) | data formatting | bytes 1048576

commit v3 on v2

v3 whole, which is shorter than its diff:
```python
import functools

import jax
import jax.numpy as jnp
from jax import lax
from jax.experimental import pallas as pl
from jax.experimental.pallas import tpu as pltpu
from jax.sharding import PartitionSpec as P

F32 = jnp.float32
BF16 = jnp.bfloat16
MESH = pl.DeviceIdType.MESH
PW = 256
LAYERS = 2
TILE = 128
NZ, NY, NX = 8, 4, 4
PLANE = NY * NX
PEERS = NZ * PLANE
CORES = 2
MEMBERS = 512
STATE = 131072
OWNED = MEMBERS // PEERS
BLOCK = STATE // CORES // PEERS
TILES = MEMBERS // TILE
LOWER = [(i, j) for i in range(TILES) for j in range(i + 1)]
HEAD = 2
HEAD_ROWS = HEAD * TILE // PLANE
GRAM_ROWS = (len(LOWER) - HEAD) * TILE // CORES // PLANE
PANEL = 16
PARTS = 8
CROSS_ROWS = MEMBERS // CORES // PLANE
CHUNK = 256
GROUPS = CHUNK // OWNED


def exact_dot(left, right):
    return jnp.dot(left, right, precision=lax.Precision.HIGHEST, preferred_element_type=F32)


def contract(left, right):
    return lax.dot_general(left, right, (((1,), (1,)), ((), ())), preferred_element_type=F32)


def repeated(tile, k):
    return jnp.broadcast_to(tile[k : k + 1, :], tile.shape)


def eliminate(a, first):
    tiles = range(PANEL // 8)
    last = first + PANEL
    sub = lax.broadcasted_iota(jnp.int32, (8, TILE), 0)
    lane = lax.broadcasted_iota(jnp.int32, (8, TILE), 1)
    rows = [a[first + 8 * t : first + 8 * t + 8, :] for t in tiles]
    own = (lane >= first) & (lane < last)
    fresh = [jnp.where(own, jnp.where(lane - first == sub + 8 * t, 1.0, 0.0), rows[t]) for t in tiles]
    cols = [
        [jnp.broadcast_to(rows[t][:, first + j : first + j + 1], (8, TILE)) for t in tiles]
        for j in range(PANEL)
    ]
    for k in range(PANEL):
        at, of = divmod(k, 8)
        pivot = cols[k]
        inverse = 1.0 / repeated(pivot[at], of)

        def reduced(column):
            row = repeated(column[at], of) * inverse
            out = [column[t] - pivot[t] * row for t in tiles]
            out[at] = jnp.where(sub == of, row, out[at])
            return out

        for j in range(k + 1, PANEL):
            cols[j] = reduced(cols[j])
        fresh = reduced(fresh)
    block = jnp.concatenate(fresh, axis=0)
    lanes = lax.broadcasted_iota(jnp.int32, (TILE, TILE), 1)
    rest = jnp.where((lanes >= first) & (lanes < last), 0.0, a)
    left = a[:, first:last]
    parts = []
    if first:
        parts.append(rest[:first] - exact_dot(left[:first], block))
    parts.append(block)
    if last < TILE:
        sums = [None] * 4
        for j in range(PANEL):
            term = jnp.broadcast_to(left[last : last + PANEL, j : j + 1], (PANEL, TILE)) * (
                jnp.broadcast_to(block[j : j + 1, :], (PANEL, TILE))
            )
            sums[j % 4] = term if sums[j % 4] is None else sums[j % 4] + term
        parts.append(rest[last : last + PANEL] - ((sums[0] + sums[1]) + (sums[2] + sums[3])))
    if last + PANEL < TILE:
        parts.append(rest[last + PANEL :] - exact_dot(left[last + PANEL :], block))
    return jnp.concatenate(parts, axis=0)


def eliminated(a, begin, end):
    for first in range(begin, end, PANEL):
        a = eliminate(a, first)
    return a


def tile_at(b):
    return slice(b * TILE, (b + 1) * TILE)


def advance(k_ref, b, inverse):
    own, following = tile_at(b), tile_at(b + 1)
    pivot = k_ref[following, following] - exact_dot(
        k_ref[following, own], exact_dot(inverse, k_ref[own, following])
    )
    rows = exact_dot(inverse, k_ref[own, :])
    cols = k_ref[:, own]
    scaled = exact_dot(cols, inverse)
    for i in range(TILES):
        for j in range(TILES):
            at = tile_at(i), tile_at(j)
            if i == b:
                k_ref[at] = inverse if j == b else rows[:, at[1]]
            elif j == b:
                k_ref[at] = -scaled[at[0], :]
            else:
                k_ref[at] = k_ref[at] - exact_dot(cols[at[0], :], rows[:, at[1]])
    return pivot


def forecast(x, up_ref, up_bias_ref, down_ref, down_bias_ref):
    for layer in range(LAYERS):
        half = 0.5 * (
            jnp.dot(x, up_ref[layer], preferred_element_type=F32) + up_bias_ref[layer : layer + 1, :]
        )
        hidden = (half + half * jnp.tanh(half)).astype(BF16)
        x = (
            x.astype(F32)
            + jnp.dot(hidden, down_ref[layer], preferred_element_type=F32)
            + down_bias_ref[layer : layer + 1, :]
        ).astype(BF16)
    return x


def wait_for(ref, sem):
    pltpu.make_async_copy(ref, ref, sem).wait()


def kernel(
    x_hbm, obs_hbm, prec_hbm, up_hbm, up_bias_hbm, down_hbm, down_bias_hbm, out_ref,
    x_own, obs_own, prec_in, prec, up, up_bias, down, down_bias, x_in, obs_in, pred, states, dev, weighted, back,
    head, head_pair, head_half, head_plane, head_z, head_all,
    gram, gram_pair, gram_half, gram_plane, gram_z, gram_all,
    cross, cross_pair, cross_half, cross_plane, cross_z, cross_all, kmat,
    load_sem, own_sem, send_sem, recv_sem,
):
    me, core = lax.axis_index("mem"), lax.axis_index("rep")
    z, q = me // PLANE, lax.rem(me, PLANE)
    y, x = q // NX, lax.rem(q, NX)

    loads = [
        pltpu.make_async_copy(src, dst, load_sem.at[i])
        for i, (src, dst) in enumerate(
            [
                (up_hbm, up), (down_hbm, down), (up_bias_hbm, up_bias), (down_bias_hbm, down_bias),
                (prec_hbm, prec_in), (x_hbm, x_own), (obs_hbm, obs_own),
            ]
        )
    ]
    own_copies = [
        pltpu.make_async_copy(x_hbm.at[me], x_in.at[me], own_sem.at[0]),
        pltpu.make_async_copy(obs_hbm.at[me], obs_in.at[me], own_sem.at[1]),
    ]

    columns = [lax.rem(x + d, NX) for d in range(NX)]
    rows_of = [lax.rem(y + d, NY) * NX for d in range(NY)]
    layers = [lax.rem(z + d, NZ) * PLANE for d in range(NZ)]
    far_first = [4, 5, 3, 6, 2, 7, 1, 0]
    plane_peers = [rows_of[b] + columns[a] for b in (2, 1, 3, 0) for a in (2, 1, 3, 0)][:-1]
    column_peers = [layers[d] + q for d in far_first[:-1]]

    def for_peers(visit):
        def one(s, carry):
            side = lax.rem(y + s // NX + 1, NY) * NX + lax.rem(x + lax.rem(s, NX) + 1, NX)
            for d in far_first:
                visit(layers[d] + side)
            return carry

        lax.fori_loop(0, PLANE - 1, one, 0)
        for target in column_peers:
            visit(target)

    barrier = pltpu.get_barrier_semaphore()

    def greet(target):
        pl.semaphore_signal(barrier, 1, device_id={"mem": target}, device_id_type=MESH)

    for_peers(greet)
    pl.semaphore_signal(barrier, 1, device_id={"rep": 1 - core}, device_id_type=MESH)
    for copy in own_copies + loads:
        copy.start()
    pl.semaphore_wait(barrier, PEERS)

    def send(src, dst, i, target):
        pltpu.make_async_remote_copy(
            src_ref=src, dst_ref=dst, send_sem=send_sem.at[i], recv_sem=recv_sem.at[i],
            device_id=target, device_id_type=MESH,
        ).start()

    def exchange(src, dst, i):
        for_peers(lambda target: send(src.at[target], dst.at[me], i, {"mem": target}))

    def to_plane(src_of, dst, i):
        for target in plane_peers:
            send(src_of(target), dst, i, {"mem": z * PLANE + target})

    def to_column(src, dst, i):
        for target in column_peers:
            send(src, dst, i, {"mem": target})

    def to_core(src, dst, i):
        send(src, dst, i, {"rep": 1 - core})

    def summed(ref):
        total = ref[0]
        for n in range(1, ref.shape[0]):
            total = total + ref[n]
        return total

    def all_but_one(ref):
        return ref.at[pl.ds(0, ref.shape[0] - 1)]

    others = pl.ds(0, PEERS - 1)
    exchange(x_hbm, x_in, 0)
    exchange(obs_hbm, obs_in, 1)

    for copy in loads:
        copy.wait()
    for c in range(BLOCK // TILE):
        prec[:, c * TILE : (c + 1) * TILE] = prec_in[pl.ds(c, PEERS, stride=BLOCK // TILE), :]

    def misfit_of(c, total):
        at = pl.ds(pl.multiple_of(c * GROUPS, GROUPS), GROUPS)
        rows = x_own[at].reshape(CHUNK, BLOCK)
        seen = obs_own[at].reshape(CHUNK, BLOCK)
        for p in range(0, BLOCK, PW):
            said = forecast(rows[:, p : p + PW], up, up_bias, down, down_bias)
            resid = (seen[:, p : p + PW].astype(F32) - said.astype(F32)).astype(BF16).astype(F32)
            square = (resid * resid).reshape(GROUPS, OWNED, PW).sum(axis=1)
            total = total + square * prec[at, p : p + PW]
        return total

    misfit = jnp.sum(
        lax.fori_loop(0, MEMBERS // CHUNK, misfit_of, jnp.zeros((GROUPS, PW), F32))
    ) / (MEMBERS * STATE)

    own_copies[0].wait()
    wait_for(x_in.at[others], recv_sem.at[0])

    def forecast_block(c, carry):
        rows = x_in[pl.ds(pl.multiple_of(c * GROUPS, GROUPS), GROUPS)].reshape(CHUNK, BLOCK)
        at = pl.ds(pl.multiple_of(c * CHUNK, CHUNK), CHUNK)
        states[at, :] = rows
        for p in range(0, BLOCK, PW):
            pred[at, p : p + PW] = forecast(rows[:, p : p + PW], up, up_bias, down, down_bias)
        return carry

    lax.fori_loop(0, MEMBERS // CHUNK, forecast_block, 0)
    prec_row = prec[pl.ds(me, 1), :]
    wide = pred[...].astype(F32)
    dev[...] = (wide - jnp.mean(wide, axis=0, keepdims=True)).astype(BF16)
    weighted[...] = (dev[...].astype(F32) * prec_row).astype(BF16)
    eye = lax.broadcasted_iota(jnp.int32, (TILE, TILE), 0) == lax.broadcasted_iota(
        jnp.int32, (TILE, TILE), 1
    )
    def lower_block(i, j):
        part = contract(weighted[tile_at(i), :], dev[tile_at(j), :]) / STATE
        return part + jnp.where(eye, misfit, 0.0) if i == j else part

    for n, (i, j) in enumerate(LOWER[:HEAD]):
        head[tile_at(n), :] = lower_block(i, j)
    to_core(head, head_pair, 2)
    for n, (i, j) in enumerate(LOWER[HEAD:]):
        gram[tile_at(n), :] = lower_block(i, j)
    half = GRAM_ROWS * PLANE
    theirs = pl.ds(pl.multiple_of((1 - core) * half, 8), half)
    mine = pl.ds(pl.multiple_of(core * half, 8), half)
    to_core(gram.at[theirs], gram_pair, 3)
    wait_for(head_pair, recv_sem.at[2])
    head_half[...] = (head[...] + head_pair[...]).reshape(PLANE, HEAD_ROWS, TILE)
    to_plane(lambda target: head_half.at[target], head_plane.at[q], 4)
    wait_for(gram_pair, recv_sem.at[3])
    gram_half[...] = (gram[mine, :] + gram_pair[...]).reshape(PLANE, GRAM_ROWS, TILE)
    to_plane(lambda target: gram_half.at[target], gram_plane.at[q], 5)

    own_copies[1].wait()
    wait_for(obs_in.at[others], recv_sem.at[1])
    for c in range(MEMBERS // CHUNK):
        at = slice(c * CHUNK, (c + 1) * CHUNK)
        seen = obs_in[c * GROUPS : (c + 1) * GROUPS].reshape(CHUNK, BLOCK)
        resid = (seen.astype(F32) - pred[at, :].astype(F32)).astype(BF16)
        cross[c] = contract(resid, weighted[...]) / STATE
    to_core(cross.at[1 - core], cross_pair, 11)

    wait_for(all_but_one(head_plane), recv_sem.at[4])
    head_plane[q] = head_half[q]
    head_z[z] = summed(head_plane)
    to_column(head_z.at[z], head_z.at[z], 6)
    wait_for(all_but_one(gram_plane), recv_sem.at[5])
    gram_plane[q] = gram_half[q]
    gram_z[z] = summed(gram_plane)
    to_column(gram_z.at[z], gram_z.at[z], 7)
    wait_for(cross_pair, recv_sem.at[11])
    cross_half[...] = (cross[core] + cross_pair[...]).reshape(PLANE, CROSS_ROWS, MEMBERS)
    to_plane(lambda target: cross_half.at[target], cross_plane.at[q], 12)
    wide = states[...].astype(F32)
    dev[...] = (wide - jnp.mean(wide, axis=0, keepdims=True)).astype(BF16)
    wait_for(all_but_one(head_z), recv_sem.at[6])
    head_all[q] = summed(head_z)
    to_plane(lambda target: head_all.at[q], head_all.at[q], 8)
    wait_for(all_but_one(gram_z), recv_sem.at[7])
    own_part = core * PLANE + q
    gram_all[own_part] = summed(gram_z)
    to_plane(lambda target: gram_all.at[own_part], gram_all.at[own_part], 9)
    wait_for(all_but_one(cross_plane), recv_sem.at[12])
    cross_plane[q] = cross_half[q]
    cross_z[z] = summed(cross_plane)
    to_column(cross_z.at[z], cross_z.at[z], 13)

    below = lax.broadcasted_iota(jnp.int32, (TILE, TILE), 0) >= lax.broadcasted_iota(
        jnp.int32, (TILE, TILE), 1
    )

    def place(lower, blocks):
        for n, (i, j) in enumerate(blocks):
            part = lower[tile_at(n), :]
            if i == j:
                part = jnp.where(below, part, part.T) + jnp.where(eye, 1e-06, 0.0)
            else:
                kmat[tile_at(j), tile_at(i)] = part.T
            kmat[tile_at(i), tile_at(j)] = part

    wait_for(all_but_one(head_all), recv_sem.at[8])
    place(head_all[...].reshape(HEAD * TILE, TILE), LOWER[:HEAD])
    inverse = eliminated(kmat[tile_at(0), tile_at(0)], 0, TILE // 2)
    core_part = pl.ds(pl.multiple_of(core * PLANE, PLANE), PLANE)
    wait_for(gram_all.at[pl.ds(0, PLANE - 1)], recv_sem.at[9])
    to_core(gram_all.at[core_part], gram_all.at[core_part], 10)
    inverse = eliminated(inverse, TILE // 2, TILE)
    wait_for(all_but_one(cross_z), recv_sem.at[13])
    cross_all[own_part] = summed(cross_z)
    to_plane(lambda target: cross_all.at[own_part], cross_all.at[own_part], 14)
    wait_for(gram_all.at[core_part], recv_sem.at[10])
    place(gram_all[...].reshape((len(LOWER) - HEAD) * TILE, TILE), LOWER[HEAD:])
    inverse = eliminated(advance(kmat, 0, inverse), 0, TILE)
    wait_for(cross_all.at[pl.ds(0, PLANE - 1)], recv_sem.at[14])
    to_core(cross_all.at[core_part], cross_all.at[core_part], 15)
    inverse = eliminated(advance(kmat, 1, inverse), 0, TILE)
    wait_for(cross_all.at[core_part], recv_sem.at[15])

    pivot = advance(kmat, 2, inverse)
    head_cols = slice(0, MEMBERS - TILE)
    tail_cols = slice(MEMBERS - TILE, MEMBERS)
    whole = cross_all[...].reshape(MEMBERS, MEMBERS)
    before = exact_dot(whole[:, head_cols], kmat[head_cols, head_cols])
    left = whole[:, tail_cols] - exact_dot(whole[:, head_cols], kmat[head_cols, tail_cols])
    inverse = eliminated(pivot, 0, TILE)
    last = exact_dot(left, inverse)
    mixing = jnp.concatenate(
        [before + exact_dot(last, kmat[tail_cols, head_cols]), last], axis=1
    ).astype(BF16)
    for c in range(MEMBERS // CHUNK):
        at = slice(c * CHUNK, (c + 1) * CHUNK)
        moved = jnp.dot(mixing[at, :], dev[...], preferred_element_type=F32)
        fresh = (states[at, :].astype(F32) + moved).astype(BF16)
        back[c * GROUPS : (c + 1) * GROUPS] = fresh.reshape(GROUPS, OWNED, BLOCK)
    home = pltpu.make_async_copy(back.at[me], out_ref.at[me], own_sem.at[2])
    home.start()
    exchange(back, out_ref, 16)
    home.wait()

    wait_for(x_hbm.at[others], send_sem.at[0])
    wait_for(obs_hbm.at[others], send_sem.at[1])
    wait_for(head_pair, send_sem.at[2])
    wait_for(gram_pair, send_sem.at[3])
    wait_for(all_but_one(head_plane), send_sem.at[4])
    wait_for(all_but_one(gram_plane), send_sem.at[5])
    wait_for(all_but_one(head_z), send_sem.at[6])
    wait_for(all_but_one(gram_z), send_sem.at[7])
    wait_for(all_but_one(head_all), send_sem.at[8])
    wait_for(gram_all.at[pl.ds(0, PLANE - 1)], send_sem.at[9])
    wait_for(gram_all.at[core_part], send_sem.at[10])
    wait_for(cross_pair, send_sem.at[11])
    wait_for(all_but_one(cross_plane), send_sem.at[12])
    wait_for(all_but_one(cross_z), send_sem.at[13])
    wait_for(cross_all.at[pl.ds(0, PLANE - 1)], send_sem.at[14])
    wait_for(cross_all.at[core_part], send_sem.at[15])
    wait_for(back.at[others], send_sem.at[16])
    wait_for(out_ref.at[others], recv_sem.at[16])


def copy_kernel(src_ref, dst_ref, sem):
    rows = PEERS // PARTS
    copies = [
        pltpu.make_async_copy(src_ref.at[pl.ds(n * rows, rows)], dst_ref.at[pl.ds(n * rows, rows)], sem.at[n])
        for n in range(PARTS)
    ]
    for copy in copies:
        copy.start()
    for copy in copies:
        copy.wait()


def body(states, observed, precision, up, up_bias, down, down_bias):
    def by_block(array):
        return array.reshape(OWNED, PEERS, BLOCK).transpose(1, 0, 2)

    hbm = pl.BlockSpec(memory_space=pltpu.HBM)
    slabs = (PEERS, OWNED, BLOCK)
    square = (MEMBERS, BLOCK)
    out = pl.pallas_call(
        kernel,
        out_shape=jax.ShapeDtypeStruct(slabs, BF16),
        in_specs=[hbm] * 7,
        out_specs=pl.BlockSpec(memory_space=pl.ANY),
        scratch_shapes=[
            pltpu.VMEM(slabs, BF16),
            pltpu.VMEM(slabs, BF16),
            pltpu.VMEM((PEERS * BLOCK // TILE, TILE), F32),
            pltpu.VMEM((PEERS, BLOCK), F32),
            pltpu.VMEM(up.shape, BF16),
            pltpu.VMEM(up_bias.shape, F32),
            pltpu.VMEM(down.shape, BF16),
            pltpu.VMEM(down_bias.shape, F32),
            pltpu.VMEM(slabs, BF16),
            pltpu.VMEM(slabs, BF16),
            pltpu.VMEM(square, BF16),
            pltpu.VMEM(square, BF16),
            pltpu.VMEM(square, BF16),
            pltpu.VMEM(square, BF16),
            pltpu.VMEM(slabs, BF16),
            pltpu.VMEM((HEAD * TILE, TILE), F32),
            pltpu.VMEM((HEAD * TILE, TILE), F32),
            pltpu.VMEM((PLANE, HEAD_ROWS, TILE), F32),
            pltpu.VMEM((PLANE, HEAD_ROWS, TILE), F32),
            pltpu.VMEM((NZ, HEAD_ROWS, TILE), F32),
            pltpu.VMEM((PLANE, HEAD_ROWS, TILE), F32),
            pltpu.VMEM(((len(LOWER) - HEAD) * TILE, TILE), F32),
            pltpu.VMEM((GRAM_ROWS * PLANE, TILE), F32),
            pltpu.VMEM((PLANE, GRAM_ROWS, TILE), F32),
            pltpu.VMEM((PLANE, GRAM_ROWS, TILE), F32),
            pltpu.VMEM((NZ, GRAM_ROWS, TILE), F32),
            pltpu.VMEM((CORES * PLANE, GRAM_ROWS, TILE), F32),
            pltpu.VMEM((CORES, MEMBERS // CORES, MEMBERS), F32),
            pltpu.VMEM((MEMBERS // CORES, MEMBERS), F32),
            pltpu.VMEM((PLANE, CROSS_ROWS, MEMBERS), F32),
            pltpu.VMEM((PLANE, CROSS_ROWS, MEMBERS), F32),
            pltpu.VMEM((NZ, CROSS_ROWS, MEMBERS), F32),
            pltpu.VMEM((CORES * PLANE, CROSS_ROWS, MEMBERS), F32),
            pltpu.VMEM((MEMBERS, MEMBERS), F32),
            pltpu.SemaphoreType.DMA((7,)),
            pltpu.SemaphoreType.DMA((3,)),
            pltpu.SemaphoreType.DMA((17,)),
            pltpu.SemaphoreType.DMA((17,)),
        ],
        compiler_params=pltpu.CompilerParams(
            collective_id=0, has_side_effects=True, vmem_limit_bytes=56 << 20
        ),
        name="ensemble_update",
    )(
        by_block(states),
        by_block(observed),
        precision.reshape(PEERS * BLOCK // TILE, TILE),
        up,
        up_bias,
        down,
        down_bias,
    )
    out = pl.pallas_call(
        copy_kernel,
        out_shape=jax.ShapeDtypeStruct(slabs, BF16),
        in_specs=[hbm],
        out_specs=hbm,
        scratch_shapes=[pltpu.SemaphoreType.DMA((PARTS,))],
        name="copy_out",
    )(out)
    return out.transpose(1, 0, 2).reshape(OWNED, PEERS * BLOCK)


def solution(mesh):
    return jax.shard_map(
        body,
        mesh=mesh,
        in_specs=(P("mem", "rep"), P("mem", "rep"), P("rep"), P(), P(), P(), P()),
        out_specs=P("mem", "rep"),
        check_vma=False,
    )
```

time: 108 us -> 112 us (1.037)
  Pallas kernels: 106 us -> 111 us
  local copies, waits for them, and re-layouts: 2.02 us -> 0 us
    pallas_call x0 -> x1, Pallas kernels: none -> 17.1 us  [body(): pl.pallas_call(copy_kernel, out_shape=jax.ShapeDtypeStruct(slabs, BF16),...]
    pallas_call x1, Pallas kernels: 106 us -> 94.3 us  [body(): pl.pallas_call(kernel, out_shape=jax.ShapeDtypeStruct(slabs, BF16), in_sp...]
    unnamed x1 -> x0, local copies, waits for them, and re-layouts: 2.02 us -> none
where the time goes in v3:
time: 112 us
  Pallas kernels  111 us (99%)
    pallas_call x1, Pallas kernels, body(): pl.pallas_call(kernel, out_shape=jax.ShapeDtypeStruct(slabs, BF16), in_sp...  94.3 us
    pallas_call x1, Pallas kernels, body(): pl.pallas_call(copy_kernel, out_shape=jax.ShapeDtypeStruct(slabs, BF16),...  17.1 us

profile of v3, /device:TPU:1, one launch (start us, length us, event | category | flops | bytes accessed | tf_op | source)
XLA Modules:
  0.0 111.5 jit_solution(16771462021692742606)
XLA Ops:
  0.0 94.3 %ensemble_update.1.src_ref = bf16[128,4,512]{2,1,0:T(4,128)(2,1)} custom-call(bf16[128,4,512]{2,1,0:T(4,128)(2,1)} %bitcast.10, bf16[128,4,512]{2,1,0:T(4,128)(2,1)} %bitcast.11, f32[512,128]{1,0:T(8,128)} %bitcast.12, bf16[2,256,1024]{2,1,0:T(8,128)(2,1)} %up_hbm.1, f32[2,1024]{1,0:T(2,128)} %up_bias_hbm.1, bf16[2,1024,256]{2,1,0:T(8,128)(2,1)} %down_hbm.1, ...), custom_call_target="tpu_custom_call" | custom-call | tf_op jit(solution)/shard_map/ensemble_update/pallas_call | solution.py:415
  94.3 17.1 %copy_out.1 = bf16[128,4,512]{2,1,0:T(4,128)(2,1)} custom-call(bf16[128,4,512]{2,1,0:T(4,128)(2,1)} %ensemble_update.1.src_ref), custom_call_target="tpu_custom_call" | custom-call | tf_op jit(solution)/shard_map/copy_out/pallas_call | solution.py:473

commit v4 on v3

--- a/solution.py
+++ b/solution.py
@@ -27,7 +27,6 @@
 HEAD_ROWS = HEAD * TILE // PLANE
 GRAM_ROWS = (len(LOWER) - HEAD) * TILE // CORES // PLANE
 PANEL = 16
-PARTS = 8
 CROSS_ROWS = MEMBERS // CORES // PLANE
 CHUNK = 256
 GROUPS = CHUNK // OWNED
@@ -146,7 +145,7 @@
     head, head_pair, head_half, head_plane, head_z, head_all,
     gram, gram_pair, gram_half, gram_plane, gram_z, gram_all,
     cross, cross_pair, cross_half, cross_plane, cross_z, cross_all, kmat,
-    load_sem, own_sem, send_sem, recv_sem,
+    load_sem, own_sem, send_sem, recv_sem, plane_in,
 ):
     me, core = lax.axis_index("mem"), lax.axis_index("rep")
     z, q = me // PLANE, lax.rem(me, PLANE)
@@ -186,14 +185,18 @@
 
     barrier = pltpu.get_barrier_semaphore()
 
-    def greet(target):
-        pl.semaphore_signal(barrier, 1, device_id={"mem": target}, device_id_type=MESH)
-
-    for_peers(greet)
+    def greet(sem, targets):
+        for target in targets:
+            pl.semaphore_signal(sem, 1, device_id={"mem": target}, device_id_type=MESH)
+
+    near = [z * PLANE + target for target in plane_peers]
+    greet(barrier, near + column_peers)
     pl.semaphore_signal(barrier, 1, device_id={"rep": 1 - core}, device_id_type=MESH)
     for copy in own_copies + loads:
         copy.start()
-    pl.semaphore_wait(barrier, PEERS)
+    pl.semaphore_wait(barrier, PLANE + NZ - 1)
+    greet(plane_in, column_peers)
+    pl.semaphore_wait(plane_in, NZ - 1)
 
     def send(src, dst, i, target):
         pltpu.make_async_remote_copy(
@@ -347,18 +350,18 @@
     wait_for(gram_all.at[core_part], recv_sem.at[10])
     place(gram_all[...].reshape((len(LOWER) - HEAD) * TILE, TILE), LOWER[HEAD:])
     inverse = eliminated(advance(kmat, 0, inverse), 0, TILE)
+    inverse = eliminated(advance(kmat, 1, inverse), 0, TILE)
     wait_for(cross_all.at[pl.ds(0, PLANE - 1)], recv_sem.at[14])
     to_core(cross_all.at[core_part], cross_all.at[core_part], 15)
-    inverse = eliminated(advance(kmat, 1, inverse), 0, TILE)
+    inverse = eliminated(advance(kmat, 2, inverse), 0, TILE // 2)
     wait_for(cross_all.at[core_part], recv_sem.at[15])
 
-    pivot = advance(kmat, 2, inverse)
     head_cols = slice(0, MEMBERS - TILE)
     tail_cols = slice(MEMBERS - TILE, MEMBERS)
     whole = cross_all[...].reshape(MEMBERS, MEMBERS)
     before = exact_dot(whole[:, head_cols], kmat[head_cols, head_cols])
     left = whole[:, tail_cols] - exact_dot(whole[:, head_cols], kmat[head_cols, tail_cols])
-    inverse = eliminated(pivot, 0, TILE)
+    inverse = eliminated(inverse, TILE // 2, TILE)
     last = exact_dot(left, inverse)
     mixing = jnp.concatenate(
         [before + exact_dot(last, kmat[tail_cols, head_cols]), last], axis=1
@@ -391,18 +394,6 @@
     wait_for(cross_all.at[core_part], send_sem.at[15])
     wait_for(back.at[others], send_sem.at[16])
     wait_for(out_ref.at[others], recv_sem.at[16])
-
-
-def copy_kernel(src_ref, dst_ref, sem):
-    rows = PEERS // PARTS
-    copies = [
-        pltpu.make_async_copy(src_ref.at[pl.ds(n * rows, rows)], dst_ref.at[pl.ds(n * rows, rows)], sem.at[n])
-        for n in range(PARTS)
-    ]
-    for copy in copies:
-        copy.start()
-    for copy in copies:
-        copy.wait()
 
 
 def body(states, observed, precision, up, up_bias, down, down_bias):
@@ -456,6 +447,7 @@
             pltpu.SemaphoreType.DMA((3,)),
             pltpu.SemaphoreType.DMA((17,)),
             pltpu.SemaphoreType.DMA((17,)),
+            pltpu.SemaphoreType.REGULAR,
         ],
         compiler_params=pltpu.CompilerParams(
             collective_id=0, has_side_effects=True, vmem_limit_bytes=56 << 20
@@ -470,14 +462,6 @@
         down,
         down_bias,
     )
-    out = pl.pallas_call(
-        copy_kernel,
-        out_shape=jax.ShapeDtypeStruct(slabs, BF16),
-        in_specs=[hbm],
-        out_specs=hbm,
-        scratch_shapes=[pltpu.SemaphoreType.DMA((PARTS,))],
-        name="copy_out",
-    )(out)
     return out.transpose(1, 0, 2).reshape(OWNED, PEERS * BLOCK)
 
 

time: 112 us -> 92.9 us (0.83)
  Pallas kernels: 111 us -> 90.8 us
  local copies, waits for them, and re-layouts: 0 us -> 2.02 us
    pallas_call x1 -> x0, Pallas kernels: 17.1 us -> none  [body(): pl.pallas_call(copy_kernel, out_shape=jax.ShapeDtypeStruct(slabs, BF16),...]
    pallas_call x1, Pallas kernels: 94.3 us -> 90.8 us  [body(): pl.pallas_call(kernel, out_shape=jax.ShapeDtypeStruct(slabs, BF16), in_sp...]
    unnamed x0 -> x1, local copies, waits for them, and re-layouts: none -> 2.02 us
where the time goes in v4:
time: 92.9 us; the launch traced here: 92.8 us
  Pallas kernels  90.8 us (98%)
  local copies, waits for them, and re-layouts  2.02 us (2%)
    pallas_call x1, Pallas kernels, body(): pl.pallas_call(kernel, out_shape=jax.ShapeDtypeStruct(slabs, BF16), in_sp...  90.8 us
    unnamed x1, local copies, waits for them, and re-layouts  2.02 us

profile of v4, /device:TPU:1, one launch (start us, length us, event | category | flops | bytes accessed | tf_op | source)
XLA Modules:
  0.0 92.8 jit_solution(9937799818028031805)
XLA Ops:
  0.0 90.8 %ensemble_update.1 = bf16[128,4,512]{2,1,0:T(4,128)(2,1)} custom-call(bf16[128,4,512]{2,1,0:T(4,128)(2,1)} %bitcast.11, bf16[128,4,512]{2,1,0:T(4,128)(2,1)} %bitcast.12, f32[512,128]{1,0:T(8,128)} %bitcast.13, bf16[2,256,1024]{2,1,0:T(8,128)(2,1)} %up_hbm.1, f32[2,1024]{1,0:T(2,128)} %up_bias_hbm.1, bf16[2,1024,256]{2,1,0:T(8,128)(2,1)} %down_hbm.1, ...), custom_call_target="tpu_custom_call" | custom-call | tf_op jit(solution)/shard_map/ensemble_update/pallas_call | solution.py:406
  90.8 2.0 %copy.9 = bf16[4,65536]{1,0:T(4,128)(2,1)} copy(bf16[4,65536]{1,0:T(4,128)(2,1)} %bitcast.10) | data formatting | bytes 1048576

commit v5 on v4

--- a/solution.py
+++ b/solution.py
@@ -299,6 +299,11 @@
         cross[c] = contract(resid, weighted[...]) / STATE
     to_core(cross.at[1 - core], cross_pair, 11)
 
+    wide = states[...].astype(F32)
+    dev[...] = (wide - jnp.mean(wide, axis=0, keepdims=True)).astype(BF16)
+    wait_for(cross_pair, recv_sem.at[11])
+    cross_half[...] = (cross[core] + cross_pair[...]).reshape(PLANE, CROSS_ROWS, MEMBERS)
+    to_plane(lambda target: cross_half.at[target], cross_plane.at[q], 12)
     wait_for(all_but_one(head_plane), recv_sem.at[4])
     head_plane[q] = head_half[q]
     head_z[z] = summed(head_plane)
@@ -307,11 +312,6 @@
     gram_plane[q] = gram_half[q]
     gram_z[z] = summed(gram_plane)
     to_column(gram_z.at[z], gram_z.at[z], 7)
-    wait_for(cross_pair, recv_sem.at[11])
-    cross_half[...] = (cross[core] + cross_pair[...]).reshape(PLANE, CROSS_ROWS, MEMBERS)
-    to_plane(lambda target: cross_half.at[target], cross_plane.at[q], 12)
-    wide = states[...].astype(F32)
-    dev[...] = (wide - jnp.mean(wide, axis=0, keepdims=True)).astype(BF16)
     wait_for(all_but_one(head_z), recv_sem.at[6])
     head_all[q] = summed(head_z)
     to_plane(lambda target: head_all.at[q], head_all.at[q], 8)

time: 92.9 us -> 91.7 us (0.987)
  Pallas kernels: 90.8 us -> 89.6 us
    pallas_call x1, Pallas kernels: 90.8 us -> 89.6 us  [body(): pl.pallas_call(kernel, out_shape=jax.ShapeDtypeStruct(slabs, BF16), in_sp...]
where the time goes in v5:
time: 91.7 us; the launch traced here: 91.6 us
  Pallas kernels  89.6 us (98%)
  local copies, waits for them, and re-layouts  2.02 us (2%)
    pallas_call x1, Pallas kernels, body(): pl.pallas_call(kernel, out_shape=jax.ShapeDtypeStruct(slabs, BF16), in_sp...  89.6 us
    unnamed x1, local copies, waits for them, and re-layouts  2.02 us

profile of v5, /device:TPU:1, one launch (start us, length us, event | category | flops | bytes accessed | tf_op | source)
XLA Modules:
  0.0 91.6 jit_solution(17113350364253337387)
XLA Ops:
  0.0 89.6 %ensemble_update.1 = bf16[128,4,512]{2,1,0:T(4,128)(2,1)} custom-call(bf16[128,4,512]{2,1,0:T(4,128)(2,1)} %bitcast.11, bf16[128,4,512]{2,1,0:T(4,128)(2,1)} %bitcast.12, f32[512,128]{1,0:T(8,128)} %bitcast.13, bf16[2,256,1024]{2,1,0:T(8,128)(2,1)} %up_hbm.1, f32[2,1024]{1,0:T(2,128)} %up_bias_hbm.1, bf16[2,1024,256]{2,1,0:T(8,128)(2,1)} %down_hbm.1, ...), custom_call_target="tpu_custom_call" | custom-call | tf_op jit(solution)/shard_map/ensemble_update/pallas_call | solution.py:406
  89.6 2.0 %copy.9 = bf16[4,65536]{1,0:T(4,128)(2,1)} copy(bf16[4,65536]{1,0:T(4,128)(2,1)} %bitcast.10) | data formatting | bytes 1048576
